TPU v7x, 32 devices: a whole 2x2x4 slice. The times are simulated.
32 devices in a mesh: section: 4 (over y, x), dp: 8 (over z, core).
Axes of the slice: x: 2, y: 2, z: 4, core: 2. Of those that a mesh axis runs over, the one named last changes fastest.
Arguments:
- patches: bfloat16 [2, 5120, 768], P(None, 'dp'), may hold values from -6 to 6
- positions: bfloat16 [878, 768], replicated, may hold values from -3 to 3
- image_sizes: int32 [2, 8, 6], P(None, 'dp'), may hold values from 0 to 3, as said below
- keep_masks: int32 [2, 8, 6, 4], P(None, 'dp'), may hold values 0 or 1
- output_grad: bfloat16 [2, 5120, 768], P(None, 'dp'), may hold values from -6 to 6
- vector_params: float32 [2, 12, 768], P(None, None, 'dp'), may hold values from -0.9 to 1.6, as said below
- attention_weights: float32 [2, 768, 3072], P(None, 'dp'), may hold values from -0.8660254 to 0.8660254
- feedforward_weights: float32 [2, 2, 768, 3072], P(None, None, 'dp'), may hold values from -0.108253175 to 0.108253175
- vector_first: float32 [2, 12, 768], P(None, None, 'dp'), may hold values from -6 to 6
- attention_first: float32 [2, 768, 3072], P(None, 'dp'), may hold values from -6 to 6
- feedforward_first: float32 [2, 2, 768, 3072], P(None, None, 'dp'), may hold values from -6 to 6
- vector_second: float32 [2, 12, 768], P(None, None, 'dp'), may hold values from 1 to 100
- attention_second: float32 [2, 768, 3072], P(None, 'dp'), may hold values from 1 to 100
- feedforward_second: float32 [2, 2, 768, 3072], P(None, None, 'dp'), may hold values from 1 to 100
- layer_rates: float32 [2], replicated, may hold values from 0.4 to 1
Outputs:
- block_out: bfloat16 [2, 5120, 768], P(None, 'dp', 'section')
- input_grad: float32 [2, 5120, 768], P(None, 'dp', 'section')
- vector_grad: float32 [2, 12, 768], P(None, None, 'dp')
- attention_grad: float32 [2, 768, 3072], P(None, 'dp')
- feedforward_grad: float32 [2, 2, 768, 3072], P(None, None, 'dp')
- vector_mean: float32 [2, 12, 768], P(None, None, 'dp')
- attention_mean: float32 [2, 768, 3072], P(None, 'dp')
- feedforward_mean: float32 [2, 2, 768, 3072], P(None, None, 'dp')
- vector_square: float32 [2, 12, 768], P(None, None, 'dp')
- attention_square: float32 [2, 768, 3072], P(None, 'dp')
- feedforward_square: float32 [2, 2, 768, 3072], P(None, None, 'dp')
- vector_step: float32 [2, 12, 768], P(None, None, 'dp')
- attention_step: float32 [2, 768, 3072], P(None, 'dp')
- feedforward_step: float32 [2, 2, 768, 3072], P(None, None, 'dp')
Inputs may be any that keep to these rules, and one draw needn't show every extreme that they name: `image_sizes`: 3 marks an empty slot. The images of the used slots, in slot order, fill the first rows of their unit and fit within its 640 rows; the rest of the unit is padding. `vector_params`: rows 0 and 5 lie near 1, the others near 0.
All inputs are finite; a program needn't handle non-finite values. No bound on the sum of `keep_masks` on one device may be relied on, other than what follows from the above.
Results may differ from a plain program's by a relative error of at most 0.015.
The roundings to bfloat16 on the way count: a program that leaves them out, or rounds other values in their place, can miss the bound.
Values may be sent and summed in bfloat16 or wider, within the bound.
No kernel may reach another device: no remote copies, remote signals or barrier semaphores. Data moves between devices by JAX's collectives and lax.ppermute only.
A program may use at most 384 MiB of HBM per device.

v0:
```python
import functools

import jax
import jax.numpy as jnp
from jax import lax
from jax.experimental import pallas as pl
from jax.experimental.pallas import tpu as pltpu
from jax.sharding import PartitionSpec as P

H = 12
HD = 64
GRID_S = 10
GRID_M = 14
GRID_L = 24

beta_one = 0.9
beta_two = 0.999
bias_one = 1.0 - 0.9**10
bias_two = 1.0 - 0.999**10
adam_eps = 1e-08
decay_rate = 0.05
drop_rate = 0.1
norm_eps = 1e-06
masked_score = -1e30
root_half = 0.7071067811865476
normal_peak = 0.3989422804014327
BF = jnp.bfloat16
F32 = jnp.float32


def image_layout(image_ids, row_count):
    small_len = GRID_S * GRID_S + 2
    middle_len = GRID_M * GRID_M + 2
    large_len = GRID_L * GRID_L + 2
    slots = image_ids.shape[0]
    lengths = jnp.where(
        image_ids == 0,
        small_len,
        jnp.where(image_ids == 1, middle_len, jnp.where(image_ids == 2, large_len, 0)),
    ).astype(jnp.int32)
    slot = jnp.arange(slots, dtype=jnp.int32)
    slot_ends = jnp.sum(jnp.where(slot[None, :] <= slot[:, None], lengths[None, :], 0), axis=1)
    slot_starts = slot_ends - lengths
    row_index = jnp.arange(row_count, dtype=jnp.int32)
    segment = jnp.sum((row_index[:, None] >= slot_ends[None, :]).astype(jnp.int32), axis=1)
    member = segment[:, None] == slot[None, :]
    first_row = jnp.sum(jnp.where(member, slot_starts[None, :], 0), axis=1)
    kind_row = jnp.sum(jnp.where(member, image_ids[None, :], 0), axis=1)
    table_start = jnp.where(
        kind_row == 0, 0, jnp.where(kind_row == 1, small_len, small_len + middle_len)
    ).astype(jnp.int32)
    in_image = segment < slots
    table_row = jnp.where(in_image, table_start + row_index - first_row, 0)
    return (segment, member, in_image, table_row)


def nn(a, b):
    return jnp.dot(a, b, preferred_element_type=F32)


def nt(a, b):
    return lax.dot_general(a, b, (((1,), (1,)), ((), ())), preferred_element_type=F32)


def tn(a, b):
    return lax.dot_general(a, b, (((0,), (0,)), ((), ())), preferred_element_type=F32)


def split3(value):
    high = value.astype(BF)
    rest = value - high.astype(F32)
    middle = rest.astype(BF)
    return high, middle, (rest - middle.astype(F32)).astype(BF)


def attention_kernel(q_ref, k_ref, v_ref, code_q_ref, code_k_ref, o_ref, lse_ref):
    low = lax.broadcasted_iota(jnp.int32, q_ref.shape, 1) < HD
    outs = []
    for half in range(2):
        own = low if half == 0 else jnp.logical_not(low)
        q = jnp.where(own, q_ref[...] * jnp.asarray(HD ** (-0.5), BF), code_q_ref[...])
        k = jnp.where(own, k_ref[...], code_k_ref[...])
        scores = nt(q, k)
        peak = jnp.max(scores, axis=-1, keepdims=True)
        e = jnp.exp(scores - peak)
        total = jnp.sum(e, axis=-1, keepdims=True)
        outs.append(nn(e.astype(BF), v_ref[...]) * (1.0 / total))
        lse_ref[:, half : half + 1] = peak + jnp.log(total)
    o_ref[...] = jnp.where(low, outs[0], outs[1]).astype(BF)


def attention_back_kernel(
    q_ref, k_ref, v_ref, do_ref, lse_ref, code_q_ref, code_k_ref, out_ref
):
    lane = lax.broadcasted_iota(jnp.int32, q_ref.shape, 1)
    low = lane < HD
    scale = HD ** (-0.5)
    dqs, dks, dvs = [], [], []
    for half in range(2):
        own = low if half == 0 else jnp.logical_not(low)
        spare = 32 + (HD if half == 0 else 0)
        q_scaled = q_ref[...] * jnp.asarray(scale, BF)
        q = jnp.where(own, q_scaled, code_q_ref[...])
        k = jnp.where(own, k_ref[...], code_k_ref[...])
        v = jnp.where(own, v_ref[...], jnp.zeros_like(v_ref[...]))
        for at, part in enumerate(split3(-lse_ref[:, half : half + 1])):
            here = lane == spare + at
            q = jnp.where(here, part, q)
            k = jnp.where(here, jnp.ones_like(k), k)
        p = jnp.exp(nt(k, q))
        dp = nt(v, do_ref[...])
        row = jnp.sum(p * dp, axis=0, keepdims=True)
        ds = (p * (dp - row)).astype(BF)
        dvs.append(nn(p.astype(BF), do_ref[...]))
        dks.append(nn(ds, q_scaled))
        dqs.append(tn(ds, k_ref[...]) * scale)
    out_ref[0] = jnp.where(low, dqs[0], dqs[1]).astype(BF)
    out_ref[1] = jnp.where(low, dks[0], dks[1]).astype(BF)
    out_ref[2] = jnp.where(low, dvs[0], dvs[1]).astype(BF)


VMEM_LIMIT = 56 * 2**20


def cost(microseconds):
    return pl.CostEstimate(flops=int(microseconds * 1.1e9), bytes_accessed=2**20, transcendentals=0)


def centered(hidden):
    center = hidden - jnp.mean(hidden, axis=-1, keepdims=True)
    inverse = lax.rsqrt(jnp.mean(center * center, axis=-1, keepdims=True) + norm_eps)
    return center * inverse, inverse


def normalize_back(normed_grad, scaled, inverse, gain):
    scaled_grad = normed_grad * gain
    mid = scaled_grad - jnp.mean(scaled_grad, axis=-1, keepdims=True)
    return inverse * (mid - scaled * jnp.mean(scaled_grad * scaled, axis=-1, keepdims=True))


def column_sum(value):
    return jnp.sum(value, axis=0, keepdims=True)


def view(weight, index):
    specs = []
    for array in weight[1]:
        if weight[0] == "full":
            _, n, _, width = array.shape
            specs.append(
                pl.BlockSpec((None, n, width // n, width), lambda p: (index(p), 0, weight[2], 0))
            )
        else:
            _, _, n, share, width = array.shape
            specs.append(
                pl.BlockSpec((None, None, n, share, width), lambda p: (weight[2], index(p), 0, 0, 0))
            )
    return specs


def cut(refs, weights):
    out = []
    for count in weights:
        out.append(refs[:count])
        refs = refs[count:]
    return (*out, refs)


def load(refs, core, held):
    n, share, width = refs[0].shape
    if len(refs) == 1:
        return refs[0][...].reshape(n * share, width)
    for turn, ref in enumerate(refs):
        side = core if turn == 0 else 1 - core
        for chip in range(n):
            row = pl.multiple_of((2 * chip + side) * share, share)
            held[pl.ds(row, share), :] = ref[chip]
    return held[...]


SMEM = pl.BlockSpec(memory_space=pltpu.SMEM)


def project_kernel(count, at_ref, hidden_ref, vec_ref, *refs):
    normed_ref, joined_ref, held = refs[count:]
    weight = load(refs[:count], at_ref[2], held)
    part = pl.program_id(0)

    @pl.when(part == 0)
    def _():
        scaled, _ = centered(hidden_ref[...].astype(F32))
        normed_ref[...] = (scaled * vec_ref[0:1] + vec_ref[1:2]).astype(BF)

    bias = jnp.where(part == 0, vec_ref[2:3], jnp.where(part == 2, vec_ref[3:4], 0.0))
    joined_ref[...] = (nn(normed_ref[...], weight) + bias).astype(BF)


def project(at, hidden, vec, wa):
    rows, width = hidden.shape
    whole = pl.BlockSpec((rows, width), lambda p: (0, 0))
    return pl.pallas_call(
        functools.partial(project_kernel, len(wa[1])),
        grid=(3,),
        in_specs=[SMEM, whole, pl.BlockSpec(vec.shape, lambda p: (0, 0))] + view(wa, lambda p: p),
        out_specs=[whole, pl.BlockSpec((None, rows, width), lambda p: (p, 0, 0))],
        out_shape=[
            jax.ShapeDtypeStruct((rows, width), BF),
            jax.ShapeDtypeStruct((3, rows, width), BF),
        ],
        compiler_params=pltpu.CompilerParams(vmem_limit_bytes=VMEM_LIMIT),
        scratch_shapes=[pltpu.VMEM((width, width), BF)],
        cost_estimate=cost(7),
        name="project",
    )(at, hidden, vec, *wa[1])


def feed_kernel(counts, at_ref, hidden_ref, o_ref, vec_ref, factor_ref, *refs):
    wo_refs, w1_refs, w2_refs, refs = cut(refs, counts)
    mid_ref, normed_ref, gb_ref, slope_ref, out_ref, total, held1, held2 = refs
    part = pl.program_id(0)
    core = at_ref[2]

    @pl.when(part == 0)
    def _():
        branch = nn(o_ref[...], load(wo_refs, core, held1)) + vec_ref[4:5]
        mid = (hidden_ref[...].astype(F32) + factor_ref[:, 0:1] * branch).astype(BF)
        mid_ref[...] = mid
        scaled, _ = centered(mid.astype(F32))
        normed_ref[...] = (scaled * vec_ref[5:6] + vec_ref[6:7]).astype(BF)
        total[...] = jnp.zeros_like(total)

    w1 = load(w1_refs, core, held1)
    w2 = load(w2_refs, core, held2)
    u = nn(normed_ref[...], w1) + vec_ref[pl.ds(8 + part, 1), :]
    cdf = 0.5 * (1.0 + lax.erf(u * root_half))
    gb = (u * cdf).astype(BF)
    gb_ref[...] = gb
    slope_ref[...] = cdf + u * jnp.exp(-0.5 * u * u) * normal_peak
    total[...] += nt(gb, w2)

    @pl.when(part == 3)
    def _():
        branch = total[...] + vec_ref[7:8]
        out_ref[...] = (mid_ref[...].astype(F32) + factor_ref[:, 1:2] * branch).astype(BF)


def feed(at, hidden, o, vec, factor, wa, w1, w2):
    rows, width = hidden.shape
    whole = pl.BlockSpec((rows, width), lambda p: (0, 0))
    part = pl.BlockSpec((None, rows, width), lambda p: (p, 0, 0))
    flat = jax.ShapeDtypeStruct((rows, width), BF)
    return pl.pallas_call(
        functools.partial(feed_kernel, [len(w[1]) for w in (wa, w1, w2)]),
        grid=(4,),
        in_specs=[
            SMEM,
            whole,
            whole,
            pl.BlockSpec(vec.shape, lambda p: (0, 0)),
            pl.BlockSpec(factor.shape, lambda p: (0, 0)),
        ]
        + view(wa, lambda p: 3)
        + view(w1, lambda p: p)
        + view(w2, lambda p: p),
        out_specs=[whole, whole, part, part, whole],
        out_shape=[
            flat,
            flat,
            jax.ShapeDtypeStruct((4, rows, width), BF),
            jax.ShapeDtypeStruct((4, rows, width), F32),
            flat,
        ],
        scratch_shapes=[pltpu.VMEM((rows, width), F32)] + [pltpu.VMEM((width, width), BF)] * 2,
        compiler_params=pltpu.CompilerParams(vmem_limit_bytes=VMEM_LIMIT),
        cost_estimate=cost(17),
        name="feed",
    )(at, hidden, o, vec, factor, *wa[1], *w1[1], *w2[1])


def feed_back_kernel(counts, at_ref, up_ref, mid_ref, vec_ref, factor_ref, slope_ref, *refs):
    wo_refs, w1_refs, w2_refs, refs = cut(refs, counts)
    eb_ref, du_ref, out_ref, eba_ref, do_ref, sums_ref, total, held1, held2 = refs
    part = pl.program_id(0)
    core = at_ref[2]

    @pl.when(part == 0)
    def _():
        eb = (factor_ref[:, 1:2] * up_ref[...].astype(F32)).astype(BF)
        eb_ref[...] = eb
        sums_ref[2:3] = column_sum(eb.astype(F32))
        total[...] = jnp.zeros_like(total)

    w1 = load(w1_refs, core, held1)
    w2 = load(w2_refs, core, held2)
    du = (nn(eb_ref[...], w2) * slope_ref[...]).astype(BF)
    du_ref[...] = du
    sums_ref[pl.ds(3 + part, 1), :] = column_sum(du.astype(F32))
    total[...] += nt(du, w1)

    @pl.when(part == 3)
    def _():
        scaled, inverse = centered(mid_ref[...].astype(F32))
        dn = total[...]
        sums_ref[0:1] = column_sum(dn * scaled)
        sums_ref[1:2] = column_sum(dn)
        up = up_ref[...].astype(F32) + normalize_back(dn, scaled, inverse, vec_ref[5:6])
        up = up.astype(BF)
        out_ref[...] = up
        eba = (factor_ref[:, 0:1] * up.astype(F32)).astype(BF)
        eba_ref[...] = eba
        sums_ref[7:8] = column_sum(eba.astype(F32))
        do_ref[...] = nt(eba, load(wo_refs, core, held1)).astype(BF)


def feed_back(at, up, mid, vec, factor, slope, wa, w1, w2):
    rows, width = up.shape
    whole = pl.BlockSpec((rows, width), lambda p: (0, 0))
    part = pl.BlockSpec((None, rows, width), lambda p: (p, 0, 0))
    flat = jax.ShapeDtypeStruct((rows, width), BF)
    return pl.pallas_call(
        functools.partial(feed_back_kernel, [len(w[1]) for w in (wa, w1, w2)]),
        grid=(4,),
        in_specs=[
            SMEM,
            whole,
            whole,
            pl.BlockSpec(vec.shape, lambda p: (0, 0)),
            pl.BlockSpec(factor.shape, lambda p: (0, 0)),
            part,
        ]
        + view(wa, lambda p: 3)
        + view(w1, lambda p: p)
        + view(w2, lambda p: p),
        out_specs=[whole, part, whole, whole, whole, pl.BlockSpec((8, width), lambda p: (0, 0))],
        out_shape=[
            flat,
            jax.ShapeDtypeStruct((4, rows, width), BF),
            flat,
            flat,
            flat,
            jax.ShapeDtypeStruct((8, width), F32),
        ],
        scratch_shapes=[pltpu.VMEM((rows, width), F32)] + [pltpu.VMEM((width, width), BF)] * 2,
        compiler_params=pltpu.CompilerParams(vmem_limit_bytes=VMEM_LIMIT),
        cost_estimate=cost(17),
        name="feed_back",
    )(at, up, mid, vec, factor, slope, *wa[1], *w1[1], *w2[1])


def project_back_kernel(count, at_ref, up_ref, hidden_ref, vec_ref, joined_ref, *refs):
    out_ref, sums_ref, total, held = refs[count:]
    part = pl.program_id(0)
    grad = nt(joined_ref[...], load(refs[:count], at_ref[2], held))
    sums_ref[pl.ds(2 + part, 1), :] = column_sum(joined_ref[...].astype(F32))

    @pl.when(part == 0)
    def _():
        total[...] = grad

    @pl.when(part > 0)
    def _():
        total[...] += grad

    @pl.when(part == 2)
    def _():
        scaled, inverse = centered(hidden_ref[...].astype(F32))
        dn = total[...]
        sums_ref[0:1] = column_sum(dn * scaled)
        sums_ref[1:2] = column_sum(dn)
        up = up_ref[...].astype(F32) + normalize_back(dn, scaled, inverse, vec_ref[0:1])
        out_ref[...] = up.astype(BF)


def project_back(at, up, hidden, vec, joined, wa):
    rows, width = up.shape
    whole = pl.BlockSpec((rows, width), lambda p: (0, 0))
    return pl.pallas_call(
        functools.partial(project_back_kernel, len(wa[1])),
        grid=(3,),
        in_specs=[
            SMEM,
            whole,
            whole,
            pl.BlockSpec(vec.shape, lambda p: (0, 0)),
            pl.BlockSpec((None, rows, width), lambda p: (p, 0, 0)),
        ]
        + view(wa, lambda p: p),
        out_specs=[whole, pl.BlockSpec((8, width), lambda p: (0, 0))],
        out_shape=[
            jax.ShapeDtypeStruct((rows, width), BF),
            jax.ShapeDtypeStruct((8, width), F32),
        ],
        scratch_shapes=[pltpu.VMEM((rows, width), F32), pltpu.VMEM((width, width), BF)],
        compiler_params=pltpu.CompilerParams(vmem_limit_bytes=VMEM_LIMIT),
        cost_estimate=cost(8),
        name="project_back",
    )(at, up, hidden, vec, joined, *wa[1])


def attention(joined, code_q, code_k):
    _, rows, width = joined.shape
    parts = [pl.BlockSpec((None, rows, 2 * HD), functools.partial(lambda n, i: (n, 0, i), n)) for n in range(3)]
    pair = pl.BlockSpec((rows, 2 * HD), lambda i: (0, i))
    whole = pl.BlockSpec((rows, 2 * HD), lambda i: (0, 0))
    return pl.pallas_call(
        attention_kernel,
        grid=(width // (2 * HD),),
        in_specs=parts + [whole, whole],
        out_specs=[pair, pl.BlockSpec((None, rows, 2), lambda i: (i, 0, 0))],
        out_shape=[
            jax.ShapeDtypeStruct((rows, width), BF),
            jax.ShapeDtypeStruct((width // (2 * HD), rows, 2), F32),
        ],
        compiler_params=pltpu.CompilerParams(vmem_limit_bytes=VMEM_LIMIT),
        cost_estimate=cost(15),
        name="attention",
    )(joined, joined, joined, code_q, code_k)


def attention_back(joined, do, lse, code_q, code_k):
    _, rows, width = joined.shape
    parts = [pl.BlockSpec((None, rows, 2 * HD), functools.partial(lambda n, i: (n, 0, i), n)) for n in range(3)]
    pair = pl.BlockSpec((rows, 2 * HD), lambda i: (0, i))
    whole = pl.BlockSpec((rows, 2 * HD), lambda i: (0, 0))
    return pl.pallas_call(
        attention_back_kernel,
        grid=(width // (2 * HD),),
        in_specs=parts + [pair, pl.BlockSpec((None, rows, 2), lambda i: (i, 0, 0)), whole, whole],
        out_specs=pl.BlockSpec((3, rows, 2 * HD), lambda i: (0, 0, i)),
        out_shape=jax.ShapeDtypeStruct((3, rows, width), BF),
        compiler_params=pltpu.CompilerParams(vmem_limit_bytes=VMEM_LIMIT),
        cost_estimate=cost(19),
        name="attention_back",
    )(joined, joined, joined, do, lse, code_q, code_k)


def which(xy, turn, at):
    s = at[0]
    quarter = jnp.where(xy == 0, s & 2, 1 + 2 * (s & 1))
    side = jnp.where(xy == 0, s & 1, s >> 1)
    return quarter, side ^ turn


def spread(product, own, keep_ref, send_ref, held):
    held[...] = product
    share = held.shape[0] // 8
    for chip in range(4):
        mine = pl.multiple_of((2 * chip + own) * share, share)
        other = pl.multiple_of((2 * chip + 1 - own) * share, share)
        keep_ref[chip, :share] = held[pl.ds(mine, share), :].astype(BF)
        send_ref[chip, :share] = held[pl.ds(other, share), :].astype(BF)


def spread_all(product, xy, turn, mine_ref, x_ref, y_ref):
    share = product.shape[0] // 8
    rows = [product[n * share : (n + 1) * share].astype(BF) for n in range(8)]
    for ref, here in (
        (mine_ref, turn == 0),
        (x_ref, jnp.logical_and(turn == 1, xy == 0)),
        (y_ref, jnp.logical_and(turn == 1, xy == 1)),
    ):

        @pl.when(here)
        def _(ref=ref):
            for n in range(8):
                ref[n] = rows[n]


def attention_weight_kernel(rows_too, at_ref, a_ref, o_ref, joined_ref, eb_ref, *rest):
    turned, held = rest[-2:]
    share = held.shape[0] // 8
    if rows_too:
        keep_ref, send_ref = rest[-4:-2]
        for chip in range(4):
            keep_ref[chip, share:] = rest[0][2 * chip + at_ref[2]]
            send_ref[chip, share:] = rest[0][2 * chip + 1 - at_ref[2]]
    xy, turn = pl.program_id(0), pl.program_id(1)
    last = which(xy, turn, at_ref)[0] == 3

    @pl.when(jnp.logical_and(turn == 0, last))
    def _():
        turned[...] = o_ref[...].T

    @pl.when(jnp.logical_and(turn == 0, jnp.logical_not(last)))
    def _():
        turned[...] = a_ref[...].T

    right = jnp.where(last, eb_ref[...], joined_ref[...])
    product = nn(turned[...], right)
    if rows_too:
        spread(product, at_ref[2], keep_ref, send_ref, held)
    else:
        spread_all(product, xy, turn, *rest[-5:-2])


def weight_outs(count, rows, width, more=0):
    share, half = width // 8 + more, width // 2
    shape = jax.ShapeDtypeStruct((2, 2, 4, count, share, half), BF)
    block = (None, None, 4, None, share, half)
    scratch = [pltpu.VMEM((width, rows), BF), pltpu.VMEM((width, half), F32)]
    return [shape, shape], block, scratch


def load_into(refs, core, target):
    if len(refs) == 1:
        n, share, width = refs[0].shape
        target[...] = refs[0][...].reshape(n * share, width)
        return target[...]
    return load(refs, core, target)


def wide_half(ref, quarter, half, columns):
    return ref[quarter, :, pl.ds(pl.multiple_of(half * columns, 128), columns)]


def feed_both_kernel(counts, at_ref, hidden_ref, o_ref, up_ref, vec_ref, factor_ref, *refs):
    wo_refs, w1_refs, w2_refs, refs = cut(refs, counts)
    out_ref, back_ref, eba_ref, do_ref, sums_ref, mine_ref, x_ref, y_ref = refs[:8]
    total, w1, w2, held, normed, mid_held, eb, gb, slope, du, turned = refs[8:]
    step = pl.program_id(0)
    core = at_ref[2]

    @pl.when(step == 0)
    def _():
        branch = nn(o_ref[...], load(wo_refs, core, held)) + vec_ref[4:5]
        mid = (hidden_ref[...].astype(F32) + factor_ref[:, 0:1] * branch).astype(BF)
        mid_held[...] = mid
        scaled, _ = centered(mid.astype(F32))
        normed[...] = (scaled * vec_ref[5:6] + vec_ref[6:7]).astype(BF)
        total[...] = jnp.zeros_like(total)

    @pl.when(step < 4)
    def _():
        u = nn(normed[...], load_into(w1_refs, core, w1.at[step])) + vec_ref[pl.ds(8 + step, 1), :]
        cdf = 0.5 * (1.0 + lax.erf(u * root_half))
        active = (u * cdf).astype(BF)
        gb[step] = active
        slope[step] = cdf + u * jnp.exp(-0.5 * u * u) * normal_peak
        total[...] += nt(active, load_into(w2_refs, core, w2.at[step]))

    @pl.when(step == 3)
    def _():
        branch = total[...] + vec_ref[7:8]
        out_ref[...] = (mid_held[...].astype(F32) + factor_ref[:, 1:2] * branch).astype(BF)
        own = (factor_ref[:, 1:2] * up_ref[...].astype(F32)).astype(BF)
        eb[...] = own
        sums_ref[2:3] = column_sum(own.astype(F32))
        total[...] = jnp.zeros_like(total)
        turned[0] = normed[...].T
        turned[1] = own.T

    @pl.when(jnp.logical_and(step >= 4, step < 8))
    def _():
        part = step - 4
        own = (nn(eb[...], w2[part]) * slope[part]).astype(BF)
        du[part] = own
        sums_ref[pl.ds(3 + part, 1), :] = column_sum(own.astype(F32))
        total[...] += nt(own, w1[part])

    @pl.when(step == 7)
    def _():
        scaled, inverse = centered(mid_held[...].astype(F32))
        dn = total[...]
        sums_ref[0:1] = column_sum(dn * scaled)
        sums_ref[1:2] = column_sum(dn)
        up = up_ref[...].astype(F32) + normalize_back(dn, scaled, inverse, vec_ref[5:6])
        up = up.astype(BF)
        back_ref[...] = up
        eba = (factor_ref[:, 0:1] * up.astype(F32)).astype(BF)
        eba_ref[...] = eba
        sums_ref[7:8] = column_sum(eba.astype(F32))
        do_ref[...] = nt(eba, load(wo_refs, core, held)).astype(BF)

    share, half = mine_ref.shape[1:]
    for mat, source in ((0, du), (1, gb)):

        @pl.when(jnp.logical_and(step >= 8 + 2 * mat, step < 10 + 2 * mat))
        def _(mat=mat, source=source):
            xy = (step - 8) % 2
            for turn in range(2):
                quarter, column = which(xy, turn, at_ref)
                product = nn(turned[mat], wide_half(source, quarter, column, half)).astype(BF)
                rows = [product[n * share : (n + 1) * share] for n in range(8)]
                for ref, here in ((mine_ref, turn == 0), (x_ref, xy == 0), (y_ref, xy == 1)):
                    if turn == 0 and ref is mine_ref:
                        for n in range(8):
                            ref[n] = rows[n]
                    elif turn == 1 and ref is not mine_ref:

                        @pl.when(here)
                        def _(ref=ref):
                            for n in range(8):
                                ref[n] = rows[n]


def feed_both(at, hidden, o, up, vec, factor, wa, w1, w2):
    rows, width = hidden.shape
    share, half = width // 8, width // 2
    whole = pl.BlockSpec((rows, width), lambda t: (0, 0))
    once = pl.BlockSpec((rows, width), lambda t: (0, 0), pipeline_mode=pl.Buffered(1))
    flat = jax.ShapeDtypeStruct((rows, width), BF)

    def mat_of(t):
        return jnp.maximum(t - 8, 0) // 2

    return pl.pallas_call(
        functools.partial(feed_both_kernel, [len(w[1]) for w in (wa, w1, w2)]),
        grid=(12,),
        in_specs=[
            SMEM,
            once,
            once,
            once,
            pl.BlockSpec(vec.shape, lambda t: (0, 0)),
            pl.BlockSpec(factor.shape, lambda t: (0, 0)),
        ]
        + view(wa, lambda t: 3)
        + view(w1, lambda t: jnp.minimum(t, 3))
        + view(w2, lambda t: jnp.minimum(t, 3)),
        out_specs=[whole] * 4
        + [
            pl.BlockSpec((8, width), lambda t: (0, 0)),
            pl.BlockSpec(
                (8, None, None, share, half), lambda t: (0, jnp.maximum(t - 8, 0) % 2, mat_of(t), 0, 0)
            ),
            pl.BlockSpec((8, None, share, half), lambda t: (0, mat_of(t), 0, 0)),
            pl.BlockSpec((8, None, share, half), lambda t: (0, mat_of(t), 0, 0)),
        ],
        out_shape=[flat] * 4
        + [
            jax.ShapeDtypeStruct((8, width), F32),
            jax.ShapeDtypeStruct((8, 2, 2, share, half), BF),
            jax.ShapeDtypeStruct((8, 2, share, half), BF),
            jax.ShapeDtypeStruct((8, 2, share, half), BF),
        ],
        scratch_shapes=[
            pltpu.VMEM((rows, width), F32),
            pltpu.VMEM((4, width, width), BF),
            pltpu.VMEM((4, width, width), BF),
            pltpu.VMEM((width, width), BF),
            pltpu.VMEM((rows, width), BF),
            pltpu.VMEM((rows, width), BF),
            pltpu.VMEM((rows, width), BF),
            pltpu.VMEM((4, rows, width), BF),
            pltpu.VMEM((4, rows, width), F32),
            pltpu.VMEM((4, rows, width), BF),
            pltpu.VMEM((2, width, rows), BF),
        ],
        compiler_params=pltpu.CompilerParams(vmem_limit_bytes=60 * 2**20),
        cost_estimate=cost(34),
        name="feed_both",
    )(at, hidden, o, up, vec, factor, *wa[1], *w1[1], *w2[1])


def feed_back_whole_kernel(
    counts, at_ref, up_ref, mid_ref, a_ref, vec_ref, factor_ref, slope_ref, gb_ref, *refs
):
    wo_refs, w1_refs, w2_refs, refs = cut(refs, counts)
    back_ref, eba_ref, do_ref, sums_ref, keep_ref, send_ref = refs[:6]
    total, held1, held2, eb, du, turned, held = refs[6:]
    step = pl.program_id(0)
    core = at_ref[2]

    @pl.when(step == 0)
    def _():
        own = (factor_ref[:, 1:2] * up_ref[...].astype(F32)).astype(BF)
        eb[...] = own
        sums_ref[2:3] = column_sum(own.astype(F32))
        total[...] = jnp.zeros_like(total)
        turned[0] = a_ref[...].T
        turned[1] = own.T

    @pl.when(step < 4)
    def _():
        own = (nn(eb[...], load(w2_refs, core, held2)) * slope_ref[...]).astype(BF)
        du[step] = own
        sums_ref[pl.ds(3 + step, 1), :] = column_sum(own.astype(F32))
        total[...] += nt(own, load(w1_refs, core, held1))

    @pl.when(step == 3)
    def _():
        scaled, inverse = centered(mid_ref[...].astype(F32))
        dn = total[...]
        sums_ref[0:1] = column_sum(dn * scaled)
        sums_ref[1:2] = column_sum(dn)
        up = up_ref[...].astype(F32) + normalize_back(dn, scaled, inverse, vec_ref[5:6])
        up = up.astype(BF)
        back_ref[...] = up
        eba = (factor_ref[:, 0:1] * up.astype(F32)).astype(BF)
        eba_ref[...] = eba
        sums_ref[7:8] = column_sum(eba.astype(F32))
        do_ref[...] = nt(eba, load(wo_refs, core, held1)).astype(BF)

    half = keep_ref.shape[-1]
    for mat in range(2):

        @pl.when(jnp.logical_and(step >= 4 + 2 * mat, step < 6 + 2 * mat))
        def _(mat=mat):
            for turn in range(2):
                quarter, column = which((step - 4) % 2, turn, at_ref)
                if mat == 0:
                    right = wide_half(du, quarter, column, half)
                else:
                    right = gb_ref[:, pl.ds(pl.multiple_of(column * half, 128), half)]
                spread(nn(turned[mat], right), core, keep_ref.at[turn], send_ref.at[turn], held)


def feed_back_whole(at, up, mid, a, vec, factor, slope, gb, wa, w1, w2):
    rows, width = up.shape
    share, half = width // 8, width // 2
    whole = pl.BlockSpec((rows, width), lambda t, at: (0, 0))
    once = pl.BlockSpec((rows, width), lambda t, at: (0, 0), pipeline_mode=pl.Buffered(1))
    flat = jax.ShapeDtypeStruct((rows, width), BF)

    def scalars_too(specs):
        return [
            pl.BlockSpec(spec.block_shape, functools.partial(lambda f, t, at: f(t), spec.index_map))
            for spec in specs
        ]

    def gb_at(t, at):
        return which(jnp.where(t == 7, 1, 0), 0, at)[0], 0, 0

    chunk = pl.BlockSpec(
        (None, 2, 4, None, share, half),
        lambda t, at: (jnp.maximum(t - 4, 0) % 2, 0, 0, jnp.maximum(t - 4, 0) // 2, 0, 0),
    )
    return pl.pallas_call(
        functools.partial(feed_back_whole_kernel, [len(w[1]) for w in (wa, w1, w2)]),
        grid_spec=pltpu.PrefetchScalarGridSpec(
            num_scalar_prefetch=1,
            grid=(8,),
            in_specs=[
                once,
                once,
                once,
                pl.BlockSpec(vec.shape, lambda t, at: (0, 0)),
                pl.BlockSpec(factor.shape, lambda t, at: (0, 0)),
                pl.BlockSpec((None, rows, width), lambda t, at: (jnp.minimum(t, 3), 0, 0)),
                pl.BlockSpec((None, rows, width), gb_at),
            ]
            + scalars_too(
                view(wa, lambda t: 3)
                + view(w1, lambda t: jnp.minimum(t, 3))
                + view(w2, lambda t: jnp.minimum(t, 3))
            ),
            out_specs=[whole] * 3 + [pl.BlockSpec((8, width), lambda t, at: (0, 0)), chunk, chunk],
            scratch_shapes=[
                pltpu.VMEM((rows, width), F32),
                pltpu.VMEM((width, width), BF),
                pltpu.VMEM((width, width), BF),
                pltpu.VMEM((rows, width), BF),
                pltpu.VMEM((4, rows, width), BF),
                pltpu.VMEM((2, width, rows), BF),
                pltpu.VMEM((width, half), F32),
            ],
        ),
        out_shape=[flat] * 3
        + [jax.ShapeDtypeStruct((8, width), F32)]
        + [jax.ShapeDtypeStruct((2, 2, 4, 2, share, half), BF)] * 2,
        compiler_params=pltpu.CompilerParams(vmem_limit_bytes=60 * 2**20),
        cost_estimate=cost(22),
        name="feed_back_whole",
    )(at, up, mid, a, vec, factor, slope, gb, *wa[1], *w1[1], *w2[1])


def owner_outs(count, rows, width, mat):
    share, half = width // 8, width // 2
    shapes = [jax.ShapeDtypeStruct((8, 2, count, share, half), BF)]
    shapes += [jax.ShapeDtypeStruct((8, count, share, half), BF)] * 2
    outs = [
        pl.BlockSpec((8, None, None, share, half), lambda *i: (0, i[-3], mat(*i), 0, 0)),
        pl.BlockSpec((8, None, share, half), lambda *i: (0, mat(*i), 0, 0)),
        pl.BlockSpec((8, None, share, half), lambda *i: (0, mat(*i), 0, 0)),
    ]
    return shapes, outs


def attention_weights_grad(at, a, o, joined, eb, vector_rows=None):
    rows, width = a.shape
    count = 1
    more = 0 if vector_rows is None else vector_rows.shape[1]
    shapes, block, scratch = weight_outs(count, rows, width, more)
    whole = pl.BlockSpec((rows, width), lambda i, j, at: (0, 0))

    def joined_at(i, j, at):
        quarter, half = which(i, j, at)
        return jnp.minimum(quarter, 2), 0, half

    if vector_rows is None:
        shapes, outs = owner_outs(count, rows, width, lambda i, j, at: 0)
        extra, extra_specs = (), []
    else:
        outs = [pl.BlockSpec(block, lambda i, j, at: (i, j, 0, 0, 0, 0))] * 2
        extra = (vector_rows,)
        extra_specs = [pl.BlockSpec(vector_rows.shape, lambda i, j, at: (0, 0, 0))]
    return pl.pallas_call(
        functools.partial(attention_weight_kernel, vector_rows is not None),
        grid_spec=pltpu.PrefetchScalarGridSpec(
            num_scalar_prefetch=1,
            grid=(2, 2),
            in_specs=[
                whole,
                whole,
                pl.BlockSpec((None, rows, width // 2), joined_at),
                pl.BlockSpec((rows, width // 2), lambda i, j, at: (0, which(i, j, at)[1])),
            ]
            + extra_specs,
            out_specs=outs,
            scratch_shapes=scratch,
        ),
        out_shape=shapes,
        compiler_params=pltpu.CompilerParams(vmem_limit_bytes=VMEM_LIMIT),
        cost_estimate=cost(8),
        name="attention_weights",
    )(at, a, o, joined, eb, *extra)


def units_kernel(*refs):
    out_ref, slot = refs[-1], 0
    for mine_ref, x_ref, y_ref in (refs[:3], refs[3:6]):
        count = x_ref.shape[0]
        for xy, got in enumerate((x_ref, y_ref)):
            total = mine_ref[xy].astype(F32) + got[...].astype(F32)
            out_ref[xy, slot : slot + count] = total.astype(BF)
        slot += count


def units_sum(*groups):
    specs, total = [], 0
    for mine, x_got, y_got in groups:
        owners, _, count, share, half = mine.shape
        one = pl.BlockSpec((None, count, share, half), lambda n: (n, 0, 0, 0))
        specs += [pl.BlockSpec((None, 2, count, share, half), lambda n: (n, 0, 0, 0, 0)), one, one]
        total += count
    return pl.pallas_call(
        units_kernel,
        grid=(owners,),
        in_specs=specs,
        out_specs=pl.BlockSpec((None, 2, total, share, half), lambda n: (n, 0, 0, 0, 0)),
        out_shape=jax.ShapeDtypeStruct((owners, 2, total, share, half), BF),
        cost_estimate=cost(6),
        name="units_sum",
    )(*[array for group in groups for array in group])


def adam_step(weight, first, second, gradient, rate, decay_on):
    mean_next = beta_one * first + (1.0 - beta_one) * gradient
    square_next = beta_two * second + (1.0 - beta_two) * gradient * gradient
    step_next = rate * (
        mean_next / bias_one / (jnp.sqrt(square_next / bias_two) + adam_eps) + decay_on * weight
    )
    return (mean_next, square_next, step_next)


def adam_update(weight, first_moment, second_moment, gradient, layer_rates, decay_on):
    rate = layer_rates.reshape((-1,) + (1,) * (weight.ndim - 1))
    return adam_step(weight, first_moment, second_moment, gradient, rate, decay_on)


def adam_kernel(layer, placed, at_ref, rate_ref, grad_ref, weight_ref, first_ref, second_ref, *rest):
    outs = rest[-4:]
    s = at_ref[0]
    half = grad_ref.shape[-1]
    order = ((0, 0), (1, 0), (0, 1), (2, 1), (2, 0), (3, 0), (1, 1), (3, 1))
    for n, (device, xy) in enumerate(order):
        at = pl.ds(n * half, half)
        gradient = grad_ref[device if placed else s ^ device, xy].astype(F32)
        new = adam_step(
            weight_ref[:, at], first_ref[:, at], second_ref[:, at], gradient, rate_ref[layer], decay_rate
        )
        for ref, value in zip(outs, (gradient,) + new):
            ref[:, at] = value


def adam(at, rates, gradient, weight, first, second, layer, slot, into):
    count = 1 if weight.ndim == 3 else weight.shape[1]
    share, columns = weight.shape[-2:]
    half = gradient.shape[-1]
    if weight.ndim == 3:
        spec = pl.BlockSpec((None, share, columns), lambda m, at, rates: (layer, 0, 0))
    else:
        spec = pl.BlockSpec((None, None, share, columns), lambda m, at, rates: (layer, m, 0, 0))
    extra = () if into is None else tuple(into)
    return pl.pallas_call(
        functools.partial(adam_kernel, layer, layer == 1),
        grid_spec=pltpu.PrefetchScalarGridSpec(
            num_scalar_prefetch=2,
            grid=(count,),
            in_specs=[
                pl.BlockSpec((4, 2, None, share, half), lambda m, at, rates: (0, 0, slot + m, 0, 0)),
                spec,
                spec,
                spec,
            ]
            + [pl.BlockSpec(memory_space=pl.ANY)] * len(extra),
            out_specs=[spec] * 4,
        ),
        out_shape=[jax.ShapeDtypeStruct(weight.shape, F32)] * 4,
        input_output_aliases={6 + n: n for n in range(len(extra))},
        compiler_params=pltpu.CompilerParams(vmem_limit_bytes=VMEM_LIMIT),
        cost_estimate=cost(6),
        name="adam",
    )(at, rates, gradient, weight, first, second, *extra)


def assemble_kernel(at_ref, own, far, x_far, y_far, d_left, d_right, out_ref):
    z, step = at_ref[1], pl.program_id(1)
    half = d_left.shape[-1]
    out_ref[z] = own[...]
    for n, source in enumerate((far, x_far, y_far)):

        @pl.when(step == n)
        def _(source=source):
            for k in range(3):
                out_ref[lax.rem(z + 3 - k, 4)] = source[k]

    @pl.when(step == 3)
    def _():
        for k in range(3):
            out_ref[lax.rem(z + 3 - k, 4), :, :half] = d_left[k]
            out_ref[lax.rem(z + 3 - k, 4), :, half:] = d_right[k]


def assemble(at, sources, first):
    count, _, share, width = sources[0].shape
    piece = pl.BlockSpec((3, None, share, width), lambda m, j, at: (0, first + m, 0, 0))
    cut = pl.BlockSpec((3, None, share, width // 2), lambda m, j, at: (0, first + m, 0, 0))
    own = pl.BlockSpec((None, None, share, width), lambda m, j, at: (m, at[0] ^ j, 0, 0))
    return pl.pallas_call(
        assemble_kernel,
        grid_spec=pltpu.PrefetchScalarGridSpec(
            num_scalar_prefetch=1,
            grid=(count, 4),
            in_specs=[own, piece, piece, piece, cut, cut],
            out_specs=pl.BlockSpec(
                (None, None, 4, share, width), lambda m, j, at: (m, at[0] ^ j, 0, 0, 0)
            ),
        ),
        out_shape=jax.ShapeDtypeStruct((count, 4, 4, share, width), BF),
        compiler_params=pltpu.CompilerParams(vmem_limit_bytes=VMEM_LIMIT),
        cost_estimate=cost(3 * count),
        name="assemble",
    )(at, *sources)


def pack_kernel(at_ref, wa_ref, wf_ref, flat_ref, a_ref, b_ref, c_ref):
    share = wa_ref.shape[1]
    a_ref[:share] = wa_ref[0].astype(BF)
    a_ref[share:] = flat_ref[...]
    for n in range(2):
        b_ref[n * share : (n + 1) * share] = wf_ref[0, n].astype(BF)
        c_ref[n * share : (n + 1) * share] = wf_ref[1, n].astype(BF)
    b_ref[2 * share :] = wa_ref[1].astype(BF)


def pack(at, wa, wf, flat):
    layers, share, columns = wa.shape
    width = columns // 4
    shapes = [(share + flat.shape[0], width), (3 * share, width), (2 * share, width)]
    return pl.pallas_call(
        pack_kernel,
        grid_spec=pltpu.PrefetchScalarGridSpec(
            num_scalar_prefetch=1,
            grid=(1,),
            in_specs=[
                pl.BlockSpec((layers, share, width), lambda i, at: (0, 0, at[0])),
                pl.BlockSpec((layers, 2, share, width), lambda i, at: (0, 0, 0, at[0])),
                pl.BlockSpec(flat.shape, lambda i, at: (0, 0)),
            ],
            out_specs=[pl.BlockSpec(shape, lambda i, at: (0, 0)) for shape in shapes],
        ),
        out_shape=[jax.ShapeDtypeStruct(shape, BF) for shape in shapes],
        cost_estimate=cost(2),
        name="pack",
    )(at, wa, wf, flat)


def cast_kernel(weight_ref, out_ref):
    out_ref[...] = weight_ref[...].astype(BF)


def cast_blocks(weight, layer):
    share, columns = weight.shape[-2:]
    count = 1 if weight.ndim == 3 else weight.shape[1]
    if weight.ndim == 3:
        spec = pl.BlockSpec((None, share, columns // 4), lambda m, q: (layer, 0, q))
    else:
        spec = pl.BlockSpec((None, None, share, columns // 4), lambda m, q: (layer, m, 0, q))
    return pl.pallas_call(
        cast_kernel,
        grid=(count, 4),
        in_specs=[spec],
        out_specs=pl.BlockSpec((None, None, share, columns // 4), lambda m, q: (m, q, 0, 0)),
        out_shape=jax.ShapeDtypeStruct((count, 4, share, columns // 4), BF),
        cost_estimate=cost(3 * count),
        name="cast",
    )(weight)


def after(value, *others):
    return lax.optimization_barrier((value,) + others)[0]


def shards(
    patches,
    positions,
    image_sizes,
    keep_masks,
    output_grad,
    vector_params,
    attention_weights,
    feedforward_weights,
    vector_first,
    attention_first,
    feedforward_first,
    vector_second,
    attention_second,
    feedforward_second,
    layer_rates,
):
    both = ("section", "dp")
    micro_count, row_count, width = patches.shape
    layers = vector_params.shape[0]
    share = attention_weights.shape[1]
    half = width // 2
    s = lax.axis_index("section")
    d = lax.axis_index("dp")
    s_low, s_high = s % 2, s // 2
    unit = s_low ^ s_high
    across = [(i, i ^ 1) for i in range(4)]
    along = [(i, i ^ 2) for i in range(4)]
    athwart = [(i, i ^ 3) for i in range(4)]
    shards_dp = lax.axis_size("dp")
    tuned = shards_dp == 8
    around = [[(i, (i + 2 * k) % 8) for i in range(8)] for k in (1, 2, 3)]
    swap = [(i, i ^ 1) for i in range(8)]
    at = jnp.stack([s, d // 2, d % 2]).astype(jnp.int32)
    z = d // 2

    def quarter(array):
        return lax.dynamic_slice_in_dim(array, s * width, width, axis=array.ndim - 1)

    if tuned:
        flat = vector_params.astype(BF).reshape(-1, share * 8)
        flat = jnp.pad(flat, ((0, 16 - flat.shape[0]), (0, 0)))
        a_sent, b_sent, c_sent = pack(at, attention_weights, feedforward_weights, flat)

        def around_z(sent):
            return [lax.ppermute(sent, "dp", route) for route in around]

        def around_xy(far):
            x_far = lax.ppermute(far, "section", across)
            y_far = lax.ppermute(far, "section", along)
            return x_far, y_far

        def around_d(x_far, y_far):
            d_left = lax.ppermute(y_far[..., :half], "section", across)
            d_right = lax.ppermute(x_far[..., half:], "section", along)
            return d_left, d_right

        def swapped(half_rows):
            return (half_rows, lax.ppermute(half_rows, "dp", swap))

        far = around_z(a_sent)
        vector_pieces = jnp.stack([flat] + [f[share:] for f in far])
        a_far = jnp.stack([f[:share] for f in far]).reshape(3, 1, share, width)
        a_far, b_sent = lax.optimization_barrier((a_far, b_sent))
        a_x, a_y = around_xy(a_far)
        wa_in, wf_in, _ = lax.optimization_barrier((attention_weights, feedforward_weights, a_far))
        a_blocks, t_blocks = cast_blocks(attention_weights, 0), cast_blocks(wa_in, 1)
        b_blocks, c_blocks = cast_blocks(feedforward_weights, 0), cast_blocks(wf_in, 1)
        b_far = jnp.stack(around_z(b_sent)).reshape(3, 3, share, width)
        a_x, a_y, b_far, c_sent, a_blocks, b_blocks, c_blocks, t_blocks = lax.optimization_barrier(
            (a_x, a_y, b_far, c_sent, a_blocks, b_blocks, c_blocks, t_blocks)
        )
        a_left, a_right = around_d(a_x, a_y)
        b_x, b_y = around_xy(b_far)
        a_halves = swapped(assemble(at, (a_blocks, a_far, a_x, a_y, a_left, a_right), 0))
        a_halves, c_sent = lax.optimization_barrier((a_halves, c_sent))
        c_far = around_z(c_sent)
        both_cores = jnp.stack([vector_pieces, lax.ppermute(vector_pieces, "dp", swap)])
        chips = (d // 2 - jnp.arange(4)) % 4
        order = jnp.where(jnp.arange(4)[:, None] == chips[None, :], 1.0, 0.0).astype(BF)
        both_cores = jnp.einsum("zk,kcrw->zcrw", order, both_cores.transpose(1, 0, 2, 3))
        ordered = jnp.where(d % 2 == 0, both_cores, both_cores[:, ::-1])
        ordered = ordered.reshape(8, -1)[:, : layers * 12 * share].reshape(8, layers, 12, share)
        vectors = ordered.transpose(1, 2, 0, 3).reshape(layers, 12, width).astype(F32)
        weights = [[("halves", a_halves, 0)], []]
    else:

        def gathered(piece):
            piece = lax.all_gather(quarter(piece).astype(BF), both, axis=0, tiled=True)
            return ("full", (piece.reshape(4, 1, width, width),), 0)

        vectors = lax.all_gather(vector_params.astype(BF), "dp", axis=2, tiled=True).astype(F32)
        weights = [
            (
                gathered(attention_weights[l]),
                gathered(feedforward_weights[l, 0]),
                gathered(feedforward_weights[l, 1]),
            )
            for l in range(layers)
        ]

    image_ids = lax.dynamic_index_in_dim(image_sizes[:, 0], unit, 0, keepdims=False)
    keep = lax.dynamic_index_in_dim(keep_masks[:, 0], unit, 0, keepdims=False)
    segment, member, inside, table_row = image_layout(image_ids, row_count)
    kept = jnp.sum(jnp.where(member[:, :, None], keep[None], 0), axis=1).astype(F32)
    factors = jnp.where(inside[:, None], kept / (1.0 - drop_rate), 1.0)
    patch_rows = lax.dynamic_index_in_dim(patches, unit, 0, keepdims=False).astype(F32)
    position_rows = jnp.take(positions, table_row, axis=0).astype(F32)
    hidden = patch_rows + jnp.where(inside[:, None], position_rows, 0.0)
    lane = jnp.arange(2 * HD, dtype=jnp.int32) % HD
    coded = lane[None, :] == segment[:, None]
    code_q = coded.astype(BF)
    code_k = jnp.where(coded | (lane[None, :] > image_sizes.shape[2]), 0.0, masked_score).astype(BF)

    saved = []
    output_rows = lax.dynamic_index_in_dim(output_grad, unit, 0, keepdims=False)
    for layer in range(layers):
        vec = vectors[layer]
        factor = factors[:, 2 * layer : 2 * layer + 2]
        a, joined = project(at, hidden, vec, weights[layer][0])
        if tuned and layer == 1:
            c_left, c_right, joined = lax.optimization_barrier((c_left, c_right, joined))
            c_halves = swapped(assemble(at, (c_blocks, c_far, c_x, c_y, c_left, c_right), 0))
            joined = after(joined, c_halves[0])
            weights[1] += [("halves", c_halves, 0), ("halves", c_halves, 1)]
        o, lse = attention(joined, code_q, code_k)
        if tuned and layer == 0:
            b_x, b_y, c_far, o = lax.optimization_barrier((b_x, b_y, c_far, o))
            b_left, b_right = around_d(b_x, b_y)
            c_far = jnp.stack(c_far).reshape(3, 2, share, width)
            c_x, c_y = around_xy(c_far)
            b_halves = swapped(assemble(at, (b_blocks, b_far, b_x, b_y, b_left, b_right), 0))
            t_blocks = after(t_blocks, b_halves[0])
            t_halves = swapped(assemble(at, (t_blocks, b_far, b_x, b_y, b_left, b_right), 2))
            o = after(o, t_halves[0])
            weights[0] += [("halves", b_halves, 0), ("halves", b_halves, 1)]
            weights[1] += [("halves", t_halves, 0)]
        wa, w1, w2 = weights[layer]
        if tuned and layer == 1:
            hidden, up1, eba1, do1, sums1, kept_feed, x_sent, y_sent = feed_both(
                at, hidden, o, output_rows, vec, factor, wa, w1, w2
            )
            saved.append((saved_hidden, a, joined, o, lse))
            break
        mid, a2, gb, slope, following = feed(at, hidden, o, vec, factor, wa, w1, w2)
        saved.append((hidden, a, joined, o, lse, mid, a2, gb, slope))
        hidden = following
        if tuned and layer == 0:
            c_x, c_y, hidden = lax.optimization_barrier((c_x, c_y, hidden))
            c_left, c_right = around_d(c_x, c_y)
            saved_hidden = hidden

    def pick(index, options):
        value = options[0]
        for n in range(1, len(options)):
            value = jnp.where(index == n, options[n], value)
        return value

    def outward(rows):
        blocks = [rows[:, i * (width // 4) : (i + 1) * (width // 4)] for i in range(4)]
        return pick(s, blocks), lax.ppermute(pick(s ^ 1, blocks), "section", across)

    def ordered_units(mine, theirs):
        return jnp.where(unit == 0, jnp.stack([mine, theirs]), jnp.stack([theirs, mine]))

    def over_units(here):
        return (
            lax.ppermute(here[0, 1], "section", across),
            lax.ppermute(here[1, 1], "section", along),
        )

    def added(kept_part, got):
        return (kept_part.astype(F32) + got.astype(F32)).astype(BF)

    def units_added(here, x_got, y_got):
        return (here[:, 0].astype(F32) + jnp.stack([x_got, y_got]).astype(F32)).astype(BF)

    def over_chips(summed):
        return [
            lax.ppermute(
                lax.dynamic_index_in_dim(summed, (z + k) % 4, 1, keepdims=False), "dp", route
            )
            for k, route in zip((1, 2, 3), around)
        ]

    def chips_added(summed, got):
        total = lax.dynamic_index_in_dim(summed, z, 1, keepdims=False).astype(F32)
        for part in got:
            total = total + part.astype(F32)
        return total.astype(BF)

    def over_sections(total):
        return [lax.ppermute(total, "section", route) for route in (across, along, athwart)]

    def joint(*values):
        return lax.optimization_barrier(values)

    def reduced_plainly(pairs):
        count = len(pairs)
        summed = []
        for xy, (side, route) in enumerate(((s_low, across), (s_high, along))):
            parts = [pair[xy].astype(BF) for pair in pairs]
            mine = [lax.dynamic_slice_in_dim(part, side * half, half, 1) for part in parts]
            other = [lax.dynamic_slice_in_dim(part, (1 - side) * half, half, 1) for part in parts]
            other = lax.ppermute(jnp.concatenate(other, axis=1), "section", route)
            summed.append((jnp.concatenate(mine, axis=1).astype(F32) + other.astype(F32)).astype(BF))
        stacked = jnp.concatenate(summed, axis=1)
        scattered = lax.psum_scatter(stacked, "dp", scatter_dimension=0, tiled=True)
        everyone = lax.all_gather(scattered, "section", axis=0, tiled=False)
        everyone = everyone.reshape(4, share, 2, count, half)
        order = ((0, 0), (1, 0), (0, 1), (2, 1), (2, 0), (3, 0), (1, 1), (3, 1))
        return [
            jnp.concatenate([everyone[dev, :, xy, mat] for dev, xy in order], axis=1).astype(F32)
            for mat in range(count)
        ]

    up = output_rows
    vector_rows = [None] * layers

    def put_rows(layer, attention_sums, feed_sums):
        vector_rows[layer] = jnp.concatenate(
            [attention_sums[0:3], attention_sums[4:5], feed_sums[7:8], feed_sums[0:7]]
        )

    def vectors_updated(vector_grad):
        return (vector_grad,) + adam_update(
            vector_params, vector_first, vector_second, vector_grad, layer_rates, 0.0
        )

    if tuned:
        wa, w1, w2 = weights[1]
        start, a, joined, o, lse = saved[1]
        up, eba, do, feed_sums = up1, eba1, do1, sums1
        do, kept_feed, x_sent, y_sent = joint(do, kept_feed, x_sent, y_sent)
        x_feed = lax.ppermute(x_sent, "section", across)
        y_feed = lax.ppermute(y_sent, "section", along)
        dqkv = attention_back(joined, do, lse, code_q, code_k)
        kept1, x_sent, y_sent = attention_weights_grad(at, a, o, dqkv, eba)
        x_feed, y_feed, kept1, x_sent, y_sent = joint(x_feed, y_feed, kept1, x_sent, y_sent)
        up = after(up, kept1)
        x_got = lax.ppermute(x_sent, "section", across)
        y_got = lax.ppermute(y_sent, "section", along)
        up, attention_sums = project_back(at, up, start, vectors[1], dqkv, wa)
        put_rows(1, attention_sums, feed_sums)
        x_got, y_got, up, hidden = joint(x_got, y_got, up, hidden)
        block_mine, block_theirs = outward(hidden)
        summed1 = units_sum((kept1, x_got, y_got), (kept_feed, x_feed, y_feed))
        total1 = lax.psum_scatter(summed1, "dp", scatter_dimension=0, tiled=True)
        up = after(up, summed1)
        wa, w1, w2 = weights[0]
        start, a, joined, o, lse, mid, a2, gb, slope = saved[0]
        up, eba, do, feed_sums, kept2, sent2 = feed_back_whole(
            at, up, mid, a2, vectors[0], factors[:, 0:2], slope, gb, wa, w1, w2
        )
        got2 = lax.ppermute(sent2, "dp", swap)
        here2 = added(kept2, got2)
        do = after(do, here2)
        x_got, y_got = over_units(here2)
        dqkv = attention_back(joined, do, lse, code_q, code_k)
        x_got, y_got, dqkv, total1 = joint(x_got, y_got, dqkv, total1)
        gradient1 = lax.all_gather(total1[0], "section", axis=0, tiled=False)
        summed2 = units_added(here2, x_got, y_got)
        dqkv = after(dqkv, summed2)
        z_got = over_chips(summed2)
        up, attention_sums = project_back(at, up, start, vectors[0], dqkv, wa)
        put_rows(0, attention_sums, feed_sums)
        rows_all = jnp.concatenate(vector_rows).astype(BF)
        lines = layers * 12 * share // half
        rows_all = rows_all.reshape(lines, half // share, 8, share).transpose(2, 0, 1, 3)
        rows_all = jnp.pad(rows_all.reshape(8, lines, half), ((0, 0), (0, 16 - lines), (0, 0)))
        dqkv, up = joint(dqkv, up)
        kept3, sent3 = attention_weights_grad(at, a, o, dqkv, eba, rows_all)
        got3 = lax.ppermute(sent3, "dp", swap)
        here3 = added(kept3, got3)
        x_got, y_got = over_units(here3)
        x_got, y_got, *z_got = joint(x_got, y_got, *z_got)
        summed3 = units_added(here3, x_got, y_got)
        z_got3 = over_chips(summed3)
        total2 = after(chips_added(summed2, z_got), summed3)
        g_got2 = over_sections(total2)
        gradient1 = after(gradient1, total2)
        attention_out = adam(
            at, layer_rates, gradient1, attention_weights, attention_first,
            attention_second, 1, 0, None,
        )
        feed_out = adam(
            at, layer_rates, gradient1, feedforward_weights, feedforward_first,
            feedforward_second, 1, 1, None,
        )
        *z_got3, attention_out0, feed_out0 = joint(*z_got3, attention_out[0], feed_out[0])
        attention_out = [attention_out0] + list(attention_out[1:])
        feed_out = [feed_out0] + list(feed_out[1:])
        total3 = chips_added(summed3, z_got3)
        g_got3 = over_sections(total3[:, :, :share])
        input_mine, input_theirs = outward(after(up, total3))
        vector_grad = total3[0, 0, share : share + lines].astype(F32)
        vector_grad = vector_grad.reshape(layers, 12, share)
        vector_out = vectors_updated(vector_grad)
        gradient2 = jnp.stack([total2] + g_got2)
        gradient2 = after(gradient2, total3)
        feed_out = adam(
            at, layer_rates, gradient2, feedforward_weights, feedforward_first,
            feedforward_second, 0, 0, feed_out,
        )
        *g_got3, feed_out0 = joint(*g_got3, feed_out[0])
        feed_out = [feed_out0] + list(feed_out[1:])
        gradient3 = jnp.stack([total3[:, :, :share]] + g_got3)
        attention_out = adam(
            at, layer_rates, gradient3, attention_weights, attention_first,
            attention_second, 0, 0, attention_out,
        )
    else:
        plain_attention, plain_feed = [None] * layers, [None] * layers
        block_mine, block_theirs = outward(hidden)

        def x_of(array):
            return jnp.where(s_high == 0, array[0], array[2])

        def y_of(array):
            return jnp.where(s_low == 0, array[1], array[3])

        for layer in reversed(range(layers)):
            wa, w1, w2 = weights[layer]
            start, a, joined, o, lse, mid, a2, gb, slope = saved[layer]
            factor = factors[:, 2 * layer : 2 * layer + 2]
            eb, du, up, eba, do, feed_sums = feed_back(
                at, up, mid, vectors[layer], factor, slope, wa, w1, w2
            )
            dqkv = attention_back(joined, do, lse, code_q, code_k)
            up, attention_sums = project_back(at, up, start, vectors[layer], dqkv, wa)
            put_rows(layer, attention_sums, feed_sums)
            all_four = jnp.concatenate([dqkv, eba[None]])
            plain_feed[layer] = jnp.stack(
                reduced_plainly(
                    [(tn(a2, x_of(du)), tn(a2, y_of(du))), (tn(eb, x_of(gb)), tn(eb, y_of(gb)))]
                )
            )
            y_left = jnp.where(s_low == 0, a, o)
            plain_attention[layer] = reduced_plainly(
                [(tn(a, x_of(all_four)), tn(y_left, y_of(all_four)))]
            )[0]
        rows_all = jnp.concatenate(vector_rows)
        rows_all = rows_all + lax.ppermute(rows_all, "section", across)
        rows_all = jnp.pad(rows_all, ((0, 128 - rows_all.shape[0]), (0, 0))).T
        vector_grad = lax.psum_scatter(rows_all, "dp", scatter_dimension=0, tiled=True)
        vector_out = vectors_updated(vector_grad[:, : layers * 12].T.reshape(layers, 12, share))
        input_mine, input_theirs = outward(up)
        gradient = jnp.stack(plain_attention)
        attention_out = (gradient,) + adam_update(
            attention_weights, attention_first, attention_second, gradient, layer_rates, decay_rate
        )
        gradient = jnp.stack(plain_feed)
        feed_out = (gradient,) + adam_update(
            feedforward_weights,
            feedforward_first,
            feedforward_second,
            gradient,
            layer_rates,
            decay_rate,
        )
    outs = [
        ordered_units(block_mine, block_theirs),
        ordered_units(input_mine, input_theirs).astype(F32),
    ]
    for group in zip(vector_out, attention_out, feed_out):
        outs.extend(group)
    return tuple(outs)


def solution(mesh):
    in_specs = (
        P(None, "dp", None),
        P(),
        P(None, "dp", None),
        P(None, "dp", None, None),
        P(None, "dp", None),
        P(None, None, "dp"),
        P(None, "dp", None),
        P(None, None, "dp", None),
        P(None, None, "dp"),
        P(None, "dp", None),
        P(None, None, "dp", None),
        P(None, None, "dp"),
        P(None, "dp", None),
        P(None, None, "dp", None),
        P(),
    )
    out_specs = (
        P(None, "dp", "section"),
        P(None, "dp", "section"),
        P(None, None, "dp"),
        P(None, "dp", None),
        P(None, None, "dp", None),
        P(None, None, "dp"),
        P(None, "dp", None),
        P(None, None, "dp", None),
        P(None, None, "dp"),
        P(None, "dp", None),
        P(None, None, "dp", None),
        P(None, None, "dp"),
        P(None, "dp", None),
        P(None, None, "dp", None),
    )
    return jax.shard_map(shards, mesh=mesh, in_specs=in_specs, out_specs=out_specs, check_vma=False)
```

profile of v0, /device:TPU:0, one launch (start us, length us, event | category | flops | bytes accessed | tf_op | source)
XLA Modules:
  0.0 489.0 jit_solution(3152783740192590221)
XLA Ops:
  54.7 15.5 %collective-permute-done.6 = bf16[288,768]{1,0:T(8,128)(2,1)S(1)} collective-permute-done((bf16[288,768]{1,0:T(8,128)(2,1)}, bf16[288,768]{1,0:T(8,128)(2,1)S(1)}, u32[]{:S(2)}, u32[]{:S(2)}) %collective-permute-start.6) | collective-permute-done | bytes 442400 | tf_op jit(solution)/shard_map/ppermute | solution.py:1050
  97.0 9.9 %collective-permute-start.13 = (bf16[192,768]{1,0:T(8,128)(2,1)}, bf16[192,768]{1,0:T(8,128)(2,1)S(1)}, u32[]{:S(2)}, u32[]{:S(2)}) collective-permute-start(bf16[192,768]{1,0:T(8,128)(2,1)} %get-tuple-element.152), channel_id=1, source_target_pairs={{0,2},{1,3},{2,4},{3,5},{4,6},{5,7},{6,0},{7,1},{8,10},{9,11},{10,... | collective-permute-start | bytes 884744 | tf_op jit(solution)/shard_map/ppermute | solution.py:1050
  109.5 7.2 %project.2 = (bf16[640,768]{1,0:T(8,128)(2,1)}, bf16[3,640,768]{2,1,0:T(8,128)(2,1)}) custom-call(s32[3]{0:T(128)} %pad_add_fusion.at_ref, f32[640,768]{1,0:T(8,128)} %convert_add_fusion.hidden_ref, f32[12,768]{1,0:T(8,128)} %squeeze.60.vec_ref, bf16[1,4,4,96,768]{4,3,2,1,0:T(8,128)(2,1)} %assemble.4.refs_0_, ...), custom_call_target="tpu_custom_call" | custom-call | flops 7699999744 | bytes 1048576 | tf_op jit(solution)/shard_map/project/pallas_call | solution.py:201
  116.7 12.5 %attention.2 = (bf16[640,768]{1,0:T(8,128)(2,1)}, f32[6,640,2]{2,1,0:T(8,128)}) custom-call(bf16[3,640,768]{2,1,0:T(8,128)(2,1)} %get-tuple-element.155.q_ref.k_ref.v_ref, bf16[3,640,768]{2,1,0:T(8,128)(2,1)} %get-tuple-element.155.q_ref.k_ref.v_ref, bf16[3,640,768]{2,1,0:T(8,128)(2,1)} %get-tuple-element.155.q_ref.k_ref.v_ref, ...), custom_call_target="tpu_custom_call" | custom-call | flops 16499999744 | bytes 1048576 | tf_op jit(solution)/shard_map/attention/pallas_call | solution.py:405
  131.6 13.7 %collective-permute-done.19.d_left = bf16[3,3,96,384]{3,2,1,0:T(8,128)(2,1)S(1)} collective-permute-done((bf16[3,3,96,384]{3,2,1,0:T(8,128)(2,1)S(1)}, bf16[3,3,96,384]{3,2,1,0:T(8,128)(2,1)S(1)}, u32[]{:S(2)}, u32[]{:S(2)}) %collective-permute-start.19) | collective-permute-done | bytes 663584 | tf_op jit(solution)/shard_map/ppermute | solution.py:1058
  147.6 8.1 %assemble.5.refs_2_.refs_4_ = bf16[2,4,4,96,768]{4,3,2,1,0:T(8,128)(2,1)} custom-call(s32[3]{0:T(128)} %pad_add_fusion.at_ref, bf16[2,4,96,768]{3,2,1,0:T(8,128)(2,1)} %cast.5.own, bf16[3,3,96,768]{3,2,1,0:T(8,128)(2,1)} %copy-done.5, bf16[3,3,96,768]{3,2,1,0:T(8,128)(2,1)} %copy-done.13, bf16[3,3,96,768]{3,2,1,0:T(8,128)(2,1)} %copy-done.14, ...), custom_call_target="tpu_custom_call" | custom-call | flops 6600000000 | bytes 1048576 | tf_op jit(solution)/shard_map/assemble/pallas_call | solution.py:930
  165.1 17.5 %feed.1 = (bf16[640,768]{1,0:T(8,128)(2,1)}, bf16[640,768]{1,0:T(8,128)(2,1)}, bf16[4,640,768]{2,1,0:T(8,128)(2,1)}, f32[4,640,768]{2,1,0:T(8,128)}, bf16[640,768]{1,0:T(8,128)(2,1)}) custom-call(s32[3]{0:T(128)} %pad_add_fusion.at_ref, f32[640,768]{1,0:T(8,128)} %convert_add_fusion.hidden_ref, bf16[640,768]{1,0:T(8,128)(2,1)} %get-tuple-element.166.o_ref, ...), custom_call_target="tpu_custom_call" | custom-call | flops 18699999232 | bytes 1048576 | tf_op jit(solution)/shard_map/feed/pallas_call | solution.py:252
  187.7 6.9 %project.3 = (bf16[640,768]{1,0:T(8,128)(2,1)}, bf16[3,640,768]{2,1,0:T(8,128)(2,1)}) custom-call(s32[3]{0:T(128)} %pad_add_fusion.at_ref, bf16[640,768]{1,0:T(8,128)(2,1)} %get-tuple-element.168.hidden_ref, f32[12,768]{1,0:T(8,128)} %squeeze.61.vec_ref, bf16[1,4,4,96,768]{4,3,2,1,0:T(8,128)(2,1)} %assemble.6.refs_0_, ...), custom_call_target="tpu_custom_call" | custom-call | flops 7699999744 | bytes 1048576 | tf_op jit(solution)/shard_map/project/pallas_call | solution.py:201
  198.6 8.1 %assemble.7.refs_2_.refs_4_ = bf16[2,4,4,96,768]{4,3,2,1,0:T(8,128)(2,1)} custom-call(s32[3]{0:T(128)} %pad_add_fusion.at_ref, bf16[2,4,96,768]{3,2,1,0:T(8,128)(2,1)} %cast.6.own, bf16[3,2,96,768]{3,2,1,0:T(8,128)(2,1)} %copy-done.7, bf16[3,2,96,768]{3,2,1,0:T(8,128)(2,1)} %copy-done.22, bf16[3,2,96,768]{3,2,1,0:T(8,128)(2,1)} %copy-done.23, ...), custom_call_target="tpu_custom_call" | custom-call | flops 6600000000 | bytes 1048576 | tf_op jit(solution)/shard_map/assemble/pallas_call | solution.py:930
  207.7 12.9 %attention.3 = (bf16[640,768]{1,0:T(8,128)(2,1)}, f32[6,640,2]{2,1,0:T(8,128)}) custom-call(bf16[3,640,768]{2,1,0:T(8,128)(2,1)} %get-tuple-element.176.q_ref.k_ref.v_ref, bf16[3,640,768]{2,1,0:T(8,128)(2,1)} %get-tuple-element.176.q_ref.k_ref.v_ref, bf16[3,640,768]{2,1,0:T(8,128)(2,1)} %get-tuple-element.176.q_ref.k_ref.v_ref, ...), custom_call_target="tpu_custom_call" | custom-call | flops 16499999744 | bytes 1048576 | tf_op jit(solution)/shard_map/attention/pallas_call | solution.py:405
  220.6 34.7 %feed_both.1 = (bf16[640,768]{1,0:T(8,128)(2,1)}, bf16[640,768]{1,0:T(8,128)(2,1)}, bf16[640,768]{1,0:T(8,128)(2,1)}, bf16[640,768]{1,0:T(8,128)(2,1)}, f32[8,76...) custom-call(s32[3]{0:T(128)} %pad_add_fusion.at_ref, ...), custom_call_target="tpu_custom_call" | custom-call | flops 37399998464 | bytes 1048576 | tf_op jit(solution)/shard_map/feed_both/pallas_call | solution.py:606
  256.9 19.0 %attention_back.2.joined_ref = bf16[3,640,768]{2,1,0:T(8,128)(2,1)} custom-call(bf16[3,640,768]{2,1,0:T(8,128)(2,1)} %get-tuple-element.176.q_ref.k_ref.v_ref, bf16[3,640,768]{2,1,0:T(8,128)(2,1)} %get-tuple-element.176.q_ref.k_ref.v_ref, bf16[3,640,768]{2,1,0:T(8,128)(2,1)} %get-tuple-element.176.q_ref.k_ref.v_ref, ...), custom_call_target="tpu_custom_call" | custom-call | flops 20899999744 | bytes 1048576 | tf_op jit(solution)/shard_map/attention_back/pallas_call | solution.py:425
  275.9 8.0 %attention_weights.2 = (bf16[8,2,1,96,384]{4,3,2,1,0:T(8,128)(2,1)}, bf16[8,1,96,384]{3,2,1,0:T(8,128)(2,1)}, bf16[8,1,96,384]{3,2,1,0:T(8,128)(2,1)}) custom-call(s32[3]{0:T(128)} %pad_add_fusion.at_ref, bf16[640,768]{1,0:T(8,128)(2,1)} %get-tuple-element.184.a_ref, bf16[640,768]{1,0:T(8,128)(2,1)} %get-tuple-element.177.o_ref, ...), custom_call_target="tpu_custom_call" | custom-call | flops 8800000000 | bytes 1048576 | tf_op jit(solution)/shard_map/attention_weights/pallas_call | solution.py:797
  286.6 8.8 %project_back.2 = (bf16[640,768]{1,0:T(8,128)(2,1)}, f32[8,768]{1,0:T(8,128)}) custom-call(s32[3]{0:T(128)} %pad_add_fusion.at_ref, bf16[640,768]{1,0:T(8,128)(2,1)} %get-tuple-element.195.up_ref, bf16[640,768]{1,0:T(8,128)(2,1)} %get-tuple-element.168.hidden_ref, f32[12,768]{1,0:T(8,128)} %squeeze.61.vec_ref, ...), custom_call_target="tpu_custom_call" | custom-call | flops 8800000000 | bytes 1048576 | tf_op jit(solution)/shard_map/project_back/pallas_call | solution.py:377
  301.2 7.2 %units_sum.1 = bf16[8,2,3,96,384]{4,3,2,1,0:T(8,128)(2,1)} custom-call(bf16[8,2,1,96,384]{4,3,2,1,0:T(8,128)(2,1)} %get-tuple-element.194.refs_0_, bf16[8,1,96,384]{3,2,1,0:T(8,128)(2,1)} %copy-done.41, bf16[8,1,96,384]{3,2,1,0:T(8,128)(2,1)} %copy-done.42, bf16[8,2,2,96,384]{4,3,2,1,0:T(8,128)(2,1)} %get-tuple-element.202.refs_3_, ...), custom_call_target="tpu_custom_call" | custom-call | flops 6600000000 | bytes 1048576 | tf_op jit(solution)/shard_map/units_sum/pallas_call | solution.py:836
  308.5 24.7 %feed_back_whole.1 = (bf16[640,768]{1,0:T(8,128)(2,1)}, bf16[640,768]{1,0:T(8,128)(2,1)}, bf16[640,768]{1,0:T(8,128)(2,1)}, f32[8,768]{1,0:T(8,128)}, bf16[2,2,4...) custom-call(s32[3]{0:T(128)} %pad_add_fusion.at_ref, bf16[640,768]{1,0:T(8,128)(2,1)} %get-tuple-element.205.up_ref, ...), custom_call_target="tpu_custom_call" | custom-call | flops 24199999488 | bytes 1048576 | tf_op jit(solution)/shard_map/feed_back_whole/pallas_call | solution.py:728
  343.2 18.9 %attention_back.3.joined_ref = bf16[3,640,768]{2,1,0:T(8,128)(2,1)} custom-call(bf16[3,640,768]{2,1,0:T(8,128)(2,1)} %get-tuple-element.155.q_ref.k_ref.v_ref, bf16[3,640,768]{2,1,0:T(8,128)(2,1)} %get-tuple-element.155.q_ref.k_ref.v_ref, bf16[3,640,768]{2,1,0:T(8,128)(2,1)} %get-tuple-element.155.q_ref.k_ref.v_ref, ...), custom_call_target="tpu_custom_call" | custom-call | flops 20899999744 | bytes 1048576 | tf_op jit(solution)/shard_map/attention_back/pallas_call | solution.py:425
  364.7 9.4 %project_back.3 = (bf16[640,768]{1,0:T(8,128)(2,1)}, f32[8,768]{1,0:T(8,128)}) custom-call(s32[3]{0:T(128)} %pad_add_fusion.at_ref, bf16[640,768]{1,0:T(8,128)(2,1)} %get-tuple-element.219.up_ref, f32[640,768]{1,0:T(8,128)} %convert_add_fusion.hidden_ref, f32[12,768]{1,0:T(8,128)} %squeeze.60.vec_ref, bf16[3,640,768]{2,1,0:T(8,128)(2,1)} %attention_back.3.joined_ref, ...), custom_call_target="tpu_custom_call" | custom-call | flops 8800000000 | bytes 1048576 | tf_op jit(solution)/shard_map/project_back/pallas_call | solution.py:377
  376.0 7.8 %attention_weights.3 = (bf16[2,2,4,1,112,384]{5,4,3,2,1,0:T(8,128)(2,1)}, bf16[2,2,4,1,112,384]{5,4,3,2,1,0:T(8,128)(2,1)}) custom-call(s32[3]{0:T(128)} %pad_add_fusion.at_ref, bf16[640,768]{1,0:T(8,128)(2,1)} %get-tuple-element.222.a_ref, bf16[640,768]{1,0:T(8,128)(2,1)} %get-tuple-element.166.o_ref, bf16[3,640,768]{2,1,0:T(8,128)(2,1)} %attention_back.3.joined_ref, ...), custom_call_target="tpu_custom_call" | custom-call | flops 8800000000 | bytes 1048576 | tf_op jit(solution)/shard_map/attention_weights/pallas_call | solution.py:797
  392.7 8.1 %collective-permute-start.37 = (bf16[2,2,96,384]{3,2,1,0:T(8,128)(2,1)}, bf16[2,2,96,384]{3,2,1,0:T(8,128)(2,1)}, u32[]{:S(2)}, u32[]{:S(2)}) collective-permute-start(bf16[2,2,96,384]{3,2,1,0:T(8,128)(2,1)} %get-tuple-element.351), channel_id=1, source_target_pairs={{0,2},{1,3},{2,4},{3,5},{4,6},{5,7},{6,0},{7,1},{8,10},{9,11},{10,... | collective-permute-start | bytes 884744 | tf_op jit(solution)/shard_map/ppermute | solution.py:1184
  409.6 10.4 %collective-permute-done.38 = bf16[2,2,96,384]{3,2,1,0:T(8,128)(2,1)} collective-permute-done((bf16[2,2,96,384]{3,2,1,0:T(8,128)(2,1)}, bf16[2,2,96,384]{3,2,1,0:T(8,128)(2,1)}, u32[]{:S(2)}, u32[]{:S(2)}) %collective-permute-start.38) | collective-permute-done | bytes 294944 | tf_op jit(solution)/shard_map/ppermute | solution.py:1184
  428.7 6.8 %collective-permute-start.40 = (bf16[2,1,112,384]{3,2,0,1:T(8,128)(2,1)S(1)}, bf16[2,1,112,384]{3,2,0,1:T(8,128)(2,1)S(1)}, u32[]{:S(2)}, u32[]{:S(2)}) collective-permute-start(bf16[2,1,112,384]{3,2,0,1:T(8,128)(2,1)S(1)} %get-tuple-element.358), channel_id=1, source_target_pairs={{0,2},{1,3},{2,4},{3,5},{4,6},{5,7},{6,0},{7,1},{8,10},{9,11},{10,... | collective-permute-start | bytes 516104 | tf_op jit(solution)/shard_map/ppermute | solution.py:1184
  443.0 7.6 %adam.5 = (f32[2,2,96,3072]{3,2,1,0:T(8,128)}, f32[2,2,96,3072]{3,2,1,0:T(8,128)}, f32[2,2,96,3072]{3,2,1,0:T(8,128)}, f32[2,2,96,3072]{3,2,1,0:T(8,128)}) custom-call(s32[3]{0:T(128)} %pad_add_fusion.at_ref, f32[2]{0:T(128)} %rate_ref.7, bf16[4,2,3,96,384]{4,3,2,1,0:T(8,128)(2,1)} %all-gather.2.cloned.1.call-done.grad_ref, f32[2,2,96,3072]{3,2,1,0:T(8,128)} %weight_ref.12, ...), custom_call_target="tpu_custom_call" | custom-call | flops 6600000000 | bytes 1048576 | tf_op jit(solution)/shard_map/adam/pallas_call | solution.py:885
  462.3 7.4 %adam.6 = (f32[2,2,96,3072]{3,2,1,0:T(8,128)}, f32[2,2,96,3072]{3,2,1,0:T(8,128)}, f32[2,2,96,3072]{3,2,1,0:T(8,128)}, f32[2,2,96,3072]{3,2,1,0:T(8,128)}) custom-call(s32[3]{0:T(128)} %pad_add_fusion.at_ref, f32[2]{0:T(128)} %rate_ref.7, ...), custom_call_target="tpu_custom_call", output_to_operand_aliasing={{0}: (6, {}), {1}: (7, {}), {2}: (8, {}), {3}: (9, {})} | custom-call | flops 6600000000 | bytes 1048576 | tf_op jit(solution)/shard_map/adam/pallas_call | solution.py:885
  (303 shorter events, 182.3 us)
Async XLA Ops:
  7.2 354.9 %reduce-scatter.2.cloned.1.call-start = ((), (), s32[]{:S(2)}) async-start(), calls=%async_computation.1 | async-start | bytes 3981312 | tf_op jit(solution)/shard_map/reduce_scatter | solution.py:1252
  12.7 22.7 %collective-permute-start.2 = (bf16[112,768]{1,0:T(8,128)(2,1)}, bf16[112,768]{1,0:T(8,128)(2,1)S(1)}, u32[]{:S(2)}, u32[]{:S(2)}) collective-permute-start(bf16[112,768]{1,0:T(8,128)(2,1)} %get-tuple-element.140), channel_id=1, source_target_pairs={{0,6},{1,7},{2,0},{3,1},{4,2},{5,3},{6,4},{7,5},{8,14},{9,15},{10,... | collective-permute-start | bytes 516104 | tf_op jit(solution)/shard_map/ppermute | solution.py:1050
  40.6 29.7 %collective-permute-start.6 = (bf16[288,768]{1,0:T(8,128)(2,1)}, bf16[288,768]{1,0:T(8,128)(2,1)S(1)}, u32[]{:S(2)}, u32[]{:S(2)}) collective-permute-start(bf16[288,768]{1,0:T(8,128)(2,1)} %get-tuple-element.143), channel_id=1, source_target_pairs={{0,4},{1,5},{2,6},{3,7},{4,0},{5,1},{6,2},{7,3},{8,12},{9,13},{10,... | collective-permute-start | bytes 1327112 | tf_op jit(solution)/shard_map/ppermute | solution.py:1050
  41.5 28.8 %collective-permute-start.7 = (bf16[288,768]{1,0:T(8,128)(2,1)}, bf16[288,768]{1,0:T(8,128)(2,1)S(1)}, u32[]{:S(2)}, u32[]{:S(2)}) collective-permute-start(bf16[288,768]{1,0:T(8,128)(2,1)} %get-tuple-element.143), channel_id=1, source_target_pairs={{0,6},{1,7},{2,0},{3,1},{4,2},{5,3},{6,4},{7,5},{8,14},{9,15},{10,... | collective-permute-start | bytes 1327112 | tf_op jit(solution)/shard_map/ppermute | solution.py:1050
  42.9 29.7 %collective-permute-start.3 = (bf16[3,1,96,768]{3,2,1,0:T(8,128)(2,1)}, bf16[3,1,96,768]{3,2,1,0:T(8,128)(2,1)}, u32[]{:S(2)}, u32[]{:S(2)}) collective-permute-start(bf16[3,1,96,768]{3,2,1,0:T(8,128)(2,1)} %maximum_bitcast_fusion.far), channel_id=1, source_target_pairs={{0,8},{8,0},{16,24},{24,16},{1,9},{9,1},{17,25},{25,17},{2,10},{10... | collective-permute-start | bytes 1327112 | tf_op jit(solution)/shard_map/ppermute | solution.py:1053
  44.4 28.2 %collective-permute-start.4 = (bf16[3,1,96,768]{3,2,1,0:T(8,128)(2,1)}, bf16[3,1,96,768]{3,2,1,0:T(8,128)(2,1)}, u32[]{:S(2)}, u32[]{:S(2)}) collective-permute-start(bf16[3,1,96,768]{3,2,1,0:T(8,128)(2,1)} %maximum_bitcast_fusion.far), channel_id=1, source_target_pairs={{0,16},{8,24},{16,0},{24,8},{1,17},{9,25},{17,1},{25,9},{2,18},{10... | collective-permute-start | bytes 1327112 | tf_op jit(solution)/shard_map/ppermute | solution.py:1054
  95.0 34.2 %collective-permute-start.8 = (bf16[3,3,96,768]{3,2,1,0:T(8,128)(2,1)S(1)}, bf16[3,3,96,768]{3,2,1,0:T(8,128)(2,1)S(1)}, u32[]{:S(2)}, u32[]{:S(2)}) collective-permute-start(bf16[3,3,96,768]{3,2,1,0:T(8,128)(2,1)S(1)} %pad_maximum_fusion.far), channel_id=1, source_target_pairs={{0,8},{8,0},{16,24},{24,16},{1,9},{9,1},{17,25},{25,17},{2,10},{10... | collective-permute-start | bytes 3981320 | tf_op jit(solution)/shard_map/ppermute | solution.py:1053
  95.5 33.7 %collective-permute-start.9 = (bf16[3,3,96,768]{3,2,1,0:T(8,128)(2,1)S(1)}, bf16[3,3,96,768]{3,2,1,0:T(8,128)(2,1)S(1)}, u32[]{:S(2)}, u32[]{:S(2)}) collective-permute-start(bf16[3,3,96,768]{3,2,1,0:T(8,128)(2,1)S(1)} %pad_maximum_fusion.far), channel_id=1, source_target_pairs={{0,16},{8,24},{16,0},{24,8},{1,17},{9,25},{17,1},{25,9},{2,18},{10... | collective-permute-start | bytes 3981320 | tf_op jit(solution)/shard_map/ppermute | solution.py:1054
  97.0 32.2 %collective-permute-start.13 = (bf16[192,768]{1,0:T(8,128)(2,1)}, bf16[192,768]{1,0:T(8,128)(2,1)S(1)}, u32[]{:S(2)}, u32[]{:S(2)}) collective-permute-start(bf16[192,768]{1,0:T(8,128)(2,1)} %get-tuple-element.152), channel_id=1, source_target_pairs={{0,2},{1,3},{2,4},{3,5},{4,6},{5,7},{6,0},{7,1},{8,10},{9,11},{10,... | collective-permute-start | bytes 884744 | tf_op jit(solution)/shard_map/ppermute | solution.py:1050
  106.9 22.3 %collective-permute-start.14 = (bf16[192,768]{1,0:T(8,128)(2,1)}, bf16[192,768]{1,0:T(8,128)(2,1)S(1)}, u32[]{:S(2)}, u32[]{:S(2)}) collective-permute-start(bf16[192,768]{1,0:T(8,128)(2,1)} %get-tuple-element.152), channel_id=1, source_target_pairs={{0,4},{1,5},{2,6},{3,7},{4,0},{5,1},{6,2},{7,3},{8,12},{9,13},{10,... | collective-permute-start | bytes 884744 | tf_op jit(solution)/shard_map/ppermute | solution.py:1050
  107.2 22.1 %collective-permute-start.15 = (bf16[192,768]{1,0:T(8,128)(2,1)}, bf16[192,768]{1,0:T(8,128)(2,1)S(1)}, u32[]{:S(2)}, u32[]{:S(2)}) collective-permute-start(bf16[192,768]{1,0:T(8,128)(2,1)} %get-tuple-element.152), channel_id=1, source_target_pairs={{0,6},{1,7},{2,0},{3,1},{4,2},{5,3},{6,4},{7,5},{8,14},{9,15},{10,... | collective-permute-start | bytes 884744 | tf_op jit(solution)/shard_map/ppermute | solution.py:1050
  161.0 26.6 %collective-permute-start.24 = (bf16[1,4,4,96,768]{4,3,2,1,0:T(8,128)(2,1)}, bf16[1,4,4,96,768]{4,3,2,1,0:T(8,128)(2,1)}, u32[]{:S(2)}, u32[]{:S(2)}) collective-permute-start(bf16[1,4,4,96,768]{4,3,2,1,0:T(8,128)(2,1)} %assemble.6.refs_0_), channel_id=1, source_target_pairs={{0,1},{1,0},{2,3},{3,2},{4,5},{5,4},{6,7},{7,6},{8,9},{9,8},{10,11... | collective-permute-start | bytes 7077896 | tf_op jit(solution)/shard_map/ppermute | solution.py:1063
  163.5 21.7 %collective-permute-start.17 = (bf16[3,2,96,768]{3,2,1,0:T(8,128)(2,1)S(1)}, bf16[3,2,96,768]{3,2,1,0:T(8,128)(2,1)S(1)}, u32[]{:S(2)}, u32[]{:S(2)}) collective-permute-start(bf16[3,2,96,768]{3,2,1,0:T(8,128)(2,1)S(1)} %pad_maximum_fusion.2.far), channel_id=1, source_target_pairs={{0,8},{8,0},{16,24},{24,16},{1,9},{9,1},{17,25},{25,17},{2,10},{10... | collective-permute-start | bytes 2654216 | tf_op jit(solution)/shard_map/ppermute | solution.py:1053
  164.6 21.3 %collective-permute-start.18 = (bf16[3,2,96,768]{3,2,1,0:T(8,128)(2,1)S(1)}, bf16[3,2,96,768]{3,2,1,0:T(8,128)(2,1)S(1)}, u32[]{:S(2)}, u32[]{:S(2)}) collective-permute-start(bf16[3,2,96,768]{3,2,1,0:T(8,128)(2,1)S(1)} %pad_maximum_fusion.2.far), channel_id=1, source_target_pairs={{0,16},{8,24},{16,0},{24,8},{1,17},{9,25},{17,1},{25,9},{2,18},{10... | collective-permute-start | bytes 2654216 | tf_op jit(solution)/shard_map/ppermute | solution.py:1054
  255.3 28.6 %collective-permute-start.26 = (bf16[8,2,96,384]{3,2,1,0:T(8,128)(2,1)}, bf16[8,2,96,384]{3,2,1,0:T(8,128)(2,1)S(1)}, u32[]{:S(2)}, u32[]{:S(2)}) collective-permute-start(bf16[8,2,96,384]{3,2,1,0:T(8,128)(2,1)} %get-tuple-element.182), channel_id=1, source_target_pairs={{0,8},{8,0},{16,24},{24,16},{1,9},{9,1},{17,25},{25,17},{2,10},{10... | collective-permute-start | bytes 3538952 | tf_op jit(solution)/shard_map/ppermute | solution.py:1239
  256.4 28.3 %collective-permute-start.27 = (bf16[8,2,96,384]{3,2,1,0:T(8,128)(2,1)}, bf16[8,2,96,384]{3,2,1,0:T(8,128)(2,1)S(1)}, u32[]{:S(2)}, u32[]{:S(2)}) collective-permute-start(bf16[8,2,96,384]{3,2,1,0:T(8,128)(2,1)} %get-tuple-element.183), channel_id=1, source_target_pairs={{0,16},{8,24},{16,0},{24,8},{1,17},{9,25},{17,1},{25,9},{2,18},{10... | collective-permute-start | bytes 3538952 | tf_op jit(solution)/shard_map/ppermute | solution.py:1240
  308.4 134.6 %all-gather.2.cloned.1.call-start = ((), (), s32[]{:S(2)}) async-start(), calls=%async_computation.2 | async-start | bytes 2211840 | tf_op jit(solution)/shard_map/all_gather | solution.py:1265
  340.6 21.5 %collective-permute-start.32 = (bf16[4,2,96,384]{3,2,1,0:T(8,128)(2,1)S(1)}, bf16[4,2,96,384]{3,2,1,0:T(8,128)(2,1)S(1)}, u32[]{:S(2)}, u32[]{:S(2)}) collective-permute-start(bf16[4,2,96,384]{3,2,1,0:T(8,128)(2,1)S(1)} %get-tuple-element.346), channel_id=1, source_target_pairs={{0,8},{8,0},{16,24},{24,16},{1,9},{9,1},{17,25},{25,17},{2,10},{10... | collective-permute-start | bytes 1769480 | tf_op jit(solution)/shard_map/ppermute | solution.py:1172
  341.8 20.3 %collective-permute-start.33 = (bf16[4,2,96,384]{3,2,1,0:T(8,128)(2,1)S(1)}, bf16[4,2,96,384]{3,2,1,0:T(8,128)(2,1)S(1)}, u32[]{:S(2)}, u32[]{:S(2)}) collective-permute-start(bf16[4,2,96,384]{3,2,1,0:T(8,128)(2,1)S(1)} %get-tuple-element.345), channel_id=1, source_target_pairs={{0,16},{8,24},{16,0},{24,8},{1,17},{9,25},{17,1},{25,9},{2,18},{10... | collective-permute-start | bytes 1769480 | tf_op jit(solution)/shard_map/ppermute | solution.py:1173
  390.2 29.8 %collective-permute-start.35 = (bf16[4,1,112,384]{3,2,0,1:T(8,128)(2,1)}, bf16[4,1,112,384]{3,2,0,1:T(8,128)(2,1)}, u32[]{:S(2)}, u32[]{:S(2)}) collective-permute-start(bf16[4,1,112,384]{3,2,0,1:T(8,128)(2,1)} %get-tuple-element.348), channel_id=1, source_target_pairs={{0,8},{8,0},{16,24},{24,16},{1,9},{9,1},{17,25},{25,17},{2,10},{10... | collective-permute-start | bytes 1032200 | tf_op jit(solution)/shard_map/ppermute | solution.py:1172
  391.2 28.8 %collective-permute-start.36 = (bf16[4,1,112,384]{3,2,0,1:T(8,128)(2,1)}, bf16[4,1,112,384]{3,2,0,1:T(8,128)(2,1)}, u32[]{:S(2)}, u32[]{:S(2)}) collective-permute-start(bf16[4,1,112,384]{3,2,0,1:T(8,128)(2,1)} %get-tuple-element.347), channel_id=1, source_target_pairs={{0,16},{8,24},{16,0},{24,8},{1,17},{9,25},{17,1},{25,9},{2,18},{10... | collective-permute-start | bytes 1032200 | tf_op jit(solution)/shard_map/ppermute | solution.py:1173
  400.8 19.2 %collective-permute-start.38 = (bf16[2,2,96,384]{3,2,1,0:T(8,128)(2,1)}, bf16[2,2,96,384]{3,2,1,0:T(8,128)(2,1)}, u32[]{:S(2)}, u32[]{:S(2)}) collective-permute-start(bf16[2,2,96,384]{3,2,1,0:T(8,128)(2,1)} %get-tuple-element.350), channel_id=1, source_target_pairs={{0,4},{1,5},{2,6},{3,7},{4,0},{5,1},{6,2},{7,3},{8,12},{9,13},{10,... | collective-permute-start | bytes 884744 | tf_op jit(solution)/shard_map/ppermute | solution.py:1184
  428.7 27.2 %collective-permute-start.40 = (bf16[2,1,112,384]{3,2,0,1:T(8,128)(2,1)S(1)}, bf16[2,1,112,384]{3,2,0,1:T(8,128)(2,1)S(1)}, u32[]{:S(2)}, u32[]{:S(2)}) collective-permute-start(bf16[2,1,112,384]{3,2,0,1:T(8,128)(2,1)S(1)} %get-tuple-element.358), channel_id=1, source_target_pairs={{0,2},{1,3},{2,4},{3,5},{4,6},{5,7},{6,0},{7,1},{8,10},{9,11},{10,... | collective-permute-start | bytes 516104 | tf_op jit(solution)/shard_map/ppermute | solution.py:1184
  435.6 20.3 %collective-permute-start.41 = (bf16[2,1,112,384]{3,2,0,1:T(8,128)(2,1)S(1)}, bf16[2,1,112,384]{3,2,0,1:T(8,128)(2,1)S(1)}, u32[]{:S(2)}, u32[]{:S(2)}) collective-permute-start(bf16[2,1,112,384]{3,2,0,1:T(8,128)(2,1)S(1)} %get-tuple-element.357), channel_id=1, source_target_pairs={{0,4},{1,5},{2,6},{3,7},{4,0},{5,1},{6,2},{7,3},{8,12},{9,13},{10,... | collective-permute-start | bytes 516104 | tf_op jit(solution)/shard_map/ppermute | solution.py:1184
  (75 other events, 994.1 us)
Sparse Core Ops, SparseCore 0:
  308.5 47.9 reduce-scatter.1
  383.9 42.2 all-gather.1
where the time goes:
time: 496 us; the launch traced here: 489 us
  Pallas kernels  268 us (54%)
  starting transfers between devices  78.5 us (16%)
  waiting for transfers between devices  70.2 us (14%)
  local copies, waits for them, and re-layouts  29.4 us (6%)
  other arithmetic  27 us (5%)
  between operations  15.4 us (3%)
    pallas_call x2, Pallas kernels, attention_back(): pl.pallas_call(attention_back_kernel, grid=(width // (2 * HD),), in_specs...  37.9 us
    pallas_call x1, Pallas kernels, feed_both(): pl.pallas_call(functools.partial(feed_both_kernel, [len(w[1]) for w in (w...  34.7 us
    pallas_call x4, Pallas kernels, assemble(): pl.pallas_call(assemble_kernel, grid_spec=pltpu.PrefetchScalarGridSpec(nu...  25.9 us
    pallas_call x4, Pallas kernels, adam(): pl.pallas_call(functools.partial(adam_kernel, layer, layer == 1), grid_sp...  25.8 us
    pallas_call x2, Pallas kernels, attention(): pl.pallas_call(attention_kernel, grid=(width // (2 * HD),), in_specs=part...  25.4 us
    pallas_call x1, Pallas kernels, feed_back_whole(): pl.pallas_call(functools.partial(feed_back_whole_kernel, [len(w[1]) for w...  24.7 us
    ppermute x6, starting transfers between devices, over_chips(): lax.ppermute(lax.dynamic_index_in_dim(summed, (z + k) % 4, 1, keepdims=Fa...  23.5 us
    ppermute x9, starting transfers between devices, around_z(): return [lax.ppermute(sent, 'dp', route) for route in around]  23.4 us
  transfers between devices with their start and end apart: 52, of which 17 were waited for; matrix products, arithmetic and copies ran while one was open for 8% of the time, Pallas kernels for 38%

commit v1 on v0

--- a/solution.py
+++ b/solution.py
@@ -120,6 +120,7 @@
 
 
 VMEM_LIMIT = 56 * 2**20
+TURNS = (1, 3, 2)
 
 
 def cost(microseconds):
@@ -904,35 +905,37 @@
     )(at, rates, gradient, weight, first, second, *extra)
 
 
-def assemble_kernel(at_ref, own, far, x_far, y_far, d_left, d_right, out_ref):
+def assemble_kernel(at_ref, own, *refs):
+    out_ref, turns = refs[-1], refs[:-1]
     z, step = at_ref[1], pl.program_id(1)
-    half = d_left.shape[-1]
     out_ref[z] = own[...]
-    for n, source in enumerate((far, x_far, y_far)):
-
-        @pl.when(step == n)
-        def _(source=source):
-            for k in range(3):
-                out_ref[lax.rem(z + 3 - k, 4)] = source[k]
-
-    @pl.when(step == 3)
-    def _():
-        for k in range(3):
-            out_ref[lax.rem(z + 3 - k, 4), :, :half] = d_left[k]
-            out_ref[lax.rem(z + 3 - k, 4), :, half:] = d_right[k]
-
-
-def assemble(at, sources, first):
-    count, _, share, width = sources[0].shape
-    piece = pl.BlockSpec((3, None, share, width), lambda m, j, at: (0, first + m, 0, 0))
-    cut = pl.BlockSpec((3, None, share, width // 2), lambda m, j, at: (0, first + m, 0, 0))
-    own = pl.BlockSpec((None, None, share, width), lambda m, j, at: (m, at[0] ^ j, 0, 0))
+    for place, k in enumerate(TURNS):
+        far, x_far, y_far, d_left, d_right = turns[5 * place : 5 * place + 5]
+        chip = lax.rem(z + 4 - k, 4)
+        half = d_left.shape[-1]
+        for n, source in enumerate((far, x_far, y_far)):
+
+            @pl.when(step == n)
+            def _(source=source, chip=chip):
+                out_ref[chip] = source[...]
+
+        @pl.when(step == 3)
+        def _(d_left=d_left, d_right=d_right, chip=chip, half=half):
+            out_ref[chip, :, :half] = d_left[...]
+            out_ref[chip, :, half:] = d_right[...]
+
+
+def assemble(at, own, turns, first):
+    count, _, share, width = own.shape
+    piece = pl.BlockSpec((share, width), lambda m, j, at: (first + m, 0))
+    part = pl.BlockSpec((share, width // 2), lambda m, j, at: (first + m, 0))
     return pl.pallas_call(
         assemble_kernel,
         grid_spec=pltpu.PrefetchScalarGridSpec(
             num_scalar_prefetch=1,
             grid=(count, 4),
-            in_specs=[own, piece, piece, piece, cut, cut],
+            in_specs=[pl.BlockSpec((None, None, share, width), lambda m, j, at: (m, at[0] ^ j, 0, 0))]
+            + [piece, piece, piece, part, part] * 3,
             out_specs=pl.BlockSpec(
                 (None, None, 4, share, width), lambda m, j, at: (m, at[0] ^ j, 0, 0, 0)
             ),
@@ -941,17 +944,17 @@
         compiler_params=pltpu.CompilerParams(vmem_limit_bytes=VMEM_LIMIT),
         cost_estimate=cost(3 * count),
         name="assemble",
-    )(at, *sources)
-
-
-def pack_kernel(at_ref, wa_ref, wf_ref, flat_ref, a_ref, b_ref, c_ref):
+    )(at, own, *[array for turn in turns for array in turn])
+
+
+def pack_kernel(at_ref, wa_ref, wf_ref, flat_ref, first_ref, second_ref, third_ref):
     share = wa_ref.shape[1]
-    a_ref[:share] = wa_ref[0].astype(BF)
-    a_ref[share:] = flat_ref[...]
+    first_ref[:share] = wa_ref[0].astype(BF)
+    first_ref[share:] = flat_ref[...]
     for n in range(2):
-        b_ref[n * share : (n + 1) * share] = wf_ref[0, n].astype(BF)
-        c_ref[n * share : (n + 1) * share] = wf_ref[1, n].astype(BF)
-    b_ref[2 * share :] = wa_ref[1].astype(BF)
+        second_ref[n * share : (n + 1) * share] = wf_ref[0, n].astype(BF)
+        third_ref[n * share : (n + 1) * share] = wf_ref[1, n].astype(BF)
+    second_ref[2 * share :] = wa_ref[1].astype(BF)
 
 
 def pack(at, wa, wf, flat):
@@ -1034,6 +1037,7 @@
     shards_dp = lax.axis_size("dp")
     tuned = shards_dp == 8
     around = [[(i, (i + 2 * k) % 8) for i in range(8)] for k in (1, 2, 3)]
+    turned = [around[k - 1] for k in TURNS]
     swap = [(i, i ^ 1) for i in range(8)]
     at = jnp.stack([s, d // 2, d % 2]).astype(jnp.int32)
     z = d // 2
@@ -1044,49 +1048,50 @@
     if tuned:
         flat = vector_params.astype(BF).reshape(-1, share * 8)
         flat = jnp.pad(flat, ((0, 16 - flat.shape[0]), (0, 0)))
-        a_sent, b_sent, c_sent = pack(at, attention_weights, feedforward_weights, flat)
-
-        def around_z(sent):
-            return [lax.ppermute(sent, "dp", route) for route in around]
+        first_sent, second_sent, third_sent = pack(at, attention_weights, feedforward_weights, flat)
+        first = lax.all_gather(first_sent, both, axis=0, tiled=False)
+        first = first.reshape(4, 8, -1, width)
+
+        def along_z(sent, route):
+            return lax.ppermute(sent, "dp", route)
 
         def around_xy(far):
-            x_far = lax.ppermute(far, "section", across)
-            y_far = lax.ppermute(far, "section", along)
-            return x_far, y_far
+            return lax.ppermute(far, "section", across), lax.ppermute(far, "section", along)
 
         def around_d(x_far, y_far):
-            d_left = lax.ppermute(y_far[..., :half], "section", across)
-            d_right = lax.ppermute(x_far[..., half:], "section", along)
+            d_left = lax.ppermute(y_far[:, :half], "section", across)
+            d_right = lax.ppermute(x_far[:, half:], "section", along)
             return d_left, d_right
 
         def swapped(half_rows):
             return (half_rows, lax.ppermute(half_rows, "dp", swap))
 
-        far = around_z(a_sent)
-        vector_pieces = jnp.stack([flat] + [f[share:] for f in far])
-        a_far = jnp.stack([f[:share] for f in far]).reshape(3, 1, share, width)
-        a_far, b_sent = lax.optimization_barrier((a_far, b_sent))
-        a_x, a_y = around_xy(a_far)
-        wa_in, wf_in, _ = lax.optimization_barrier((attention_weights, feedforward_weights, a_far))
-        a_blocks, t_blocks = cast_blocks(attention_weights, 0), cast_blocks(wa_in, 1)
-        b_blocks, c_blocks = cast_blocks(feedforward_weights, 0), cast_blocks(wf_in, 1)
-        b_far = jnp.stack(around_z(b_sent)).reshape(3, 3, share, width)
-        a_x, a_y, b_far, c_sent, a_blocks, b_blocks, c_blocks, t_blocks = lax.optimization_barrier(
-            (a_x, a_y, b_far, c_sent, a_blocks, b_blocks, c_blocks, t_blocks)
+        fars, turns = [], []
+        sent = second_sent
+        for route in turned:
+            far = along_z(sent, route)
+            if fars:
+                far, x_far, y_far = lax.optimization_barrier((far, *pending))
+                turns.append((fars[-1], x_far, y_far))
+            far, sent = lax.optimization_barrier((far, sent))
+            pending = around_xy(far)
+            fars.append(far)
+        b_blocks = cast_blocks(feedforward_weights, 0)
+        t_blocks, c_blocks = cast_blocks(attention_weights, 1), cast_blocks(feedforward_weights, 1)
+        diagonals = [around_d(*turn[1:]) for turn in turns]
+        x_far, y_far, *diagonals = lax.optimization_barrier((*pending, *diagonals))
+        turns.append((fars[-1], x_far, y_far))
+        diagonals.append(around_d(x_far, y_far))
+        third_sent = after(third_sent, far)
+        c_fars = [along_z(third_sent, route) for route in turned]
+        first, b_blocks, t_blocks, c_blocks = lax.optimization_barrier(
+            (first, b_blocks, t_blocks, c_blocks)
         )
-        a_left, a_right = around_d(a_x, a_y)
-        b_x, b_y = around_xy(b_far)
-        a_halves = swapped(assemble(at, (a_blocks, a_far, a_x, a_y, a_left, a_right), 0))
-        a_halves, c_sent = lax.optimization_barrier((a_halves, c_sent))
-        c_far = around_z(c_sent)
-        both_cores = jnp.stack([vector_pieces, lax.ppermute(vector_pieces, "dp", swap)])
-        chips = (d // 2 - jnp.arange(4)) % 4
-        order = jnp.where(jnp.arange(4)[:, None] == chips[None, :], 1.0, 0.0).astype(BF)
-        both_cores = jnp.einsum("zk,kcrw->zcrw", order, both_cores.transpose(1, 0, 2, 3))
-        ordered = jnp.where(d % 2 == 0, both_cores, both_cores[:, ::-1])
-        ordered = ordered.reshape(8, -1)[:, : layers * 12 * share].reshape(8, layers, 12, share)
+        turns = [(*turn, *diagonal) for turn, diagonal in zip(turns, diagonals)]
+        ordered = first[0, :, share:].reshape(8, -1)[:, : layers * 12 * share]
+        ordered = ordered.reshape(8, layers, 12, share)
         vectors = ordered.transpose(1, 2, 0, 3).reshape(layers, 12, width).astype(F32)
-        weights = [[("halves", a_halves, 0)], []]
+        weights = [[("full", (first,), 0)], []]
     else:
 
         def gathered(piece):
@@ -1124,21 +1129,23 @@
         a, joined = project(at, hidden, vec, weights[layer][0])
         if tuned and layer == 1:
             c_left, c_right, joined = lax.optimization_barrier((c_left, c_right, joined))
-            c_halves = swapped(assemble(at, (c_blocks, c_far, c_x, c_y, c_left, c_right), 0))
+            c_turns = [
+                tuple(array[2 * share * n : 2 * share * (n + 1)] for array in (c_all, c_x, c_y, c_left, c_right))
+                for n in range(3)
+            ]
+            c_halves = swapped(assemble(at, c_blocks, c_turns, 0))
             joined = after(joined, c_halves[0])
             weights[1] += [("halves", c_halves, 0), ("halves", c_halves, 1)]
         o, lse = attention(joined, code_q, code_k)
         if tuned and layer == 0:
-            b_x, b_y, c_far, o = lax.optimization_barrier((b_x, b_y, c_far, o))
-            b_left, b_right = around_d(b_x, b_y)
-            c_far = jnp.stack(c_far).reshape(3, 2, share, width)
-            c_x, c_y = around_xy(c_far)
-            b_halves = swapped(assemble(at, (b_blocks, b_far, b_x, b_y, b_left, b_right), 0))
-            t_blocks = after(t_blocks, b_halves[0])
-            t_halves = swapped(assemble(at, (t_blocks, b_far, b_x, b_y, b_left, b_right), 2))
-            o = after(o, t_halves[0])
+            o, *c_fars = lax.optimization_barrier((o, *c_fars))
+            c_all = jnp.concatenate(c_fars)
+            c_x, c_y = around_xy(c_all)
+            b_halves = swapped(assemble(at, after(b_blocks, o), turns, 0))
+            t_halves = swapped(assemble(at, after(t_blocks, b_halves[0]), turns, 2))
             weights[0] += [("halves", b_halves, 0), ("halves", b_halves, 1)]
             weights[1] += [("halves", t_halves, 0)]
+            o = after(o, t_halves[0])
         wa, w1, w2 = weights[layer]
         if tuned and layer == 1:
             hidden, up1, eba1, do1, sums1, kept_feed, x_sent, y_sent = feed_both(
@@ -1246,16 +1253,17 @@
         y_got = lax.ppermute(y_sent, "section", along)
         up, attention_sums = project_back(at, up, start, vectors[1], dqkv, wa)
         put_rows(1, attention_sums, feed_sums)
-        x_got, y_got, up, hidden = joint(x_got, y_got, up, hidden)
-        block_mine, block_theirs = outward(hidden)
+        x_got, y_got, up = joint(x_got, y_got, up)
         summed1 = units_sum((kept1, x_got, y_got), (kept_feed, x_feed, y_feed))
         total1 = lax.psum_scatter(summed1, "dp", scatter_dimension=0, tiled=True)
-        up = after(up, summed1)
+        up, summed1, hidden = joint(up, summed1, hidden)
+        block_mine, block_theirs = outward(hidden)
         wa, w1, w2 = weights[0]
         start, a, joined, o, lse, mid, a2, gb, slope = saved[0]
         up, eba, do, feed_sums, kept2, sent2 = feed_back_whole(
             at, up, mid, a2, vectors[0], factors[:, 0:2], slope, gb, wa, w1, w2
         )
+        sent2, kept2, do, block_theirs = joint(sent2, kept2, do, block_theirs)
         got2 = lax.ppermute(sent2, "dp", swap)
         here2 = added(kept2, got2)
         do = after(do, here2)
@@ -1272,8 +1280,10 @@
         lines = layers * 12 * share // half
         rows_all = rows_all.reshape(lines, half // share, 8, share).transpose(2, 0, 1, 3)
         rows_all = jnp.pad(rows_all.reshape(8, lines, half), ((0, 0), (0, 16 - lines), (0, 0)))
-        dqkv, up = joint(dqkv, up)
+        dqkv, up, gradient1, *z_got = joint(dqkv, up, gradient1, *z_got)
+        input_mine, input_theirs = outward(up)
         kept3, sent3 = attention_weights_grad(at, a, o, dqkv, eba, rows_all)
+        kept3, sent3, input_theirs = joint(kept3, sent3, input_theirs)
         got3 = lax.ppermute(sent3, "dp", swap)
         here3 = added(kept3, got3)
         x_got, y_got = over_units(here3)
@@ -1281,12 +1291,13 @@
         summed3 = units_added(here3, x_got, y_got)
         z_got3 = over_chips(summed3)
         total2 = after(chips_added(summed2, z_got), summed3)
-        g_got2 = over_sections(total2)
         gradient1 = after(gradient1, total2)
         attention_out = adam(
             at, layer_rates, gradient1, attention_weights, attention_first,
             attention_second, 1, 0, None,
         )
+        total2, gradient1 = joint(after(total2, attention_out[0]), gradient1)
+        g_got2 = over_sections(total2)
         feed_out = adam(
             at, layer_rates, gradient1, feedforward_weights, feedforward_first,
             feedforward_second, 1, 1, None,
@@ -1296,7 +1307,6 @@
         feed_out = [feed_out0] + list(feed_out[1:])
         total3 = chips_added(summed3, z_got3)
         g_got3 = over_sections(total3[:, :, :share])
-        input_mine, input_theirs = outward(after(up, total3))
         vector_grad = total3[0, 0, share : share + lines].astype(F32)
         vector_grad = vector_grad.reshape(layers, 12, share)
         vector_out = vectors_updated(vector_grad)

time: 496 us -> 479 us (0.966)
  starting transfers between devices: 78.5 us -> 58.2 us
  waiting for transfers between devices: 70.2 us -> 88.9 us
  Pallas kernels: 268 us -> 260 us
    ppermute x6, starting transfers between devices: 23.5 us -> 9.3 us  [over_chips(): lax.ppermute(lax.dynamic_index_in_dim(summed, (z + k) % 4, 1, keepdims=Fa...]
    all_gather x0 -> x1, waiting for transfers between devices: none -> 8.55 us  [shards(): first = lax.all_gather(first_sent, both, axis=0, tiled=False)]
    ppermute x22, starting transfers between devices: 37.5 us -> 29.4 us  [the longest x6 11.2 us: along_z(): return lax.ppermute(sent, 'dp', route)]
    ppermute x6, waiting for transfers between devices: 14.7 us -> 8.59 us  [over_chips(): lax.ppermute(lax.dynamic_index_in_dim(summed, (z + k) % 4, 1, keepdims=Fa...]
    slice x6 -> x10, local copies, waits for them, and re-layouts: 2.42 us -> 7.94 us  [the longest x2 3.35 us: shards(): array[2 * share * n:2 * share * (n + 1)]]
    pallas_call x4 -> x3, Pallas kernels: 25.9 us -> 21.9 us  [assemble(): pl.pallas_call(assemble_kernel, grid_spec=pltpu.PrefetchScalarGridSpec(nu...]
    pallas_call x4 -> x3, Pallas kernels: 17.7 us -> 14.4 us  [cast_blocks(): pl.pallas_call(cast_kernel, grid=(count, 4), in_specs=[spec], out_specs=p...]
    unnamed x101 -> x82, local copies, waits for them, and re-layouts: 10.8 us -> 9.35 us
  transfers between devices with their start and end apart: 52 -> 52, of which waited for: 17 -> 19; matrix products, arithmetic and copies ran while one was open for 8% -> 8% of each run, Pallas kernels for 38% -> 39%
where the time goes in v1:
time: 479 us; the launch traced here: 474 us
  Pallas kernels  260 us (54%)
  waiting for transfers between devices  88.9 us (19%)
  starting transfers between devices  58.2 us (12%)
  local copies, waits for them, and re-layouts  29.4 us (6%)
  other arithmetic  22.6 us (5%)
  between operations  14.8 us (3%)
    pallas_call x2, Pallas kernels, attention_back(): pl.pallas_call(attention_back_kernel, grid=(width // (2 * HD),), in_specs...  38.2 us
    pallas_call x1, Pallas kernels, feed_both(): pl.pallas_call(functools.partial(feed_both_kernel, [len(w[1]) for w in (w...  34.7 us
    pallas_call x4, Pallas kernels, adam(): pl.pallas_call(functools.partial(adam_kernel, layer, layer == 1), grid_sp...  25.6 us
    pallas_call x2, Pallas kernels, attention(): pl.pallas_call(attention_kernel, grid=(width // (2 * HD),), in_specs=part...  25.2 us
    ppermute x6, waiting for transfers between devices, along_z(): return lax.ppermute(sent, 'dp', route)  24.9 us
    pallas_call x1, Pallas kernels, feed_back_whole(): pl.pallas_call(functools.partial(feed_back_whole_kernel, [len(w[1]) for w...  24.5 us
    ppermute x4, waiting for transfers between devices, around_d(): d_right = lax.ppermute(x_far[:, half:], 'section', along)  22 us
    pallas_call x3, Pallas kernels, assemble(): pl.pallas_call(assemble_kernel, grid_spec=pltpu.PrefetchScalarGridSpec(nu...  21.9 us
  transfers between devices with their start and end apart: 52, of which 19 were waited for; matrix products, arithmetic and copies ran while one was open for 8% of the time, Pallas kernels for 39%

profile of v1, /device:TPU:0, one launch (start us, length us, event | category | flops | bytes accessed | tf_op | source)
XLA Modules:
  0.0 473.7 jit_solution(1229492582857129821)
XLA Ops:
  16.1 5.5 %cast.3.own = bf16[2,4,96,768]{3,2,1,0:T(8,128)(2,1)} custom-call(f32[2,2,96,3072]{3,2,1,0:T(8,128)} %weight_ref.12), custom_call_target="tpu_custom_call" | custom-call | flops 6600000000 | bytes 1048576 | tf_op jit(solution)/shard_map/cast/pallas_call | solution.py:993
  21.6 5.6 %cast.5.own = bf16[2,4,96,768]{3,2,1,0:T(8,128)(2,1)} custom-call(f32[2,2,96,3072]{3,2,1,0:T(8,128)} %weight_ref.12), custom_call_target="tpu_custom_call" | custom-call | flops 6600000000 | bytes 1048576 | tf_op jit(solution)/shard_map/cast/pallas_call | solution.py:993
  52.6 21.2 %collective-permute-done.4.refs_10_ = bf16[288,768]{1,0:T(8,128)(2,1)} collective-permute-done((bf16[288,768]{1,0:T(8,128)(2,1)S(1)}, bf16[288,768]{1,0:T(8,128)(2,1)}, u32[]{:S(2)}, u32[]{:S(2)}) %collective-permute-start.4) | collective-permute-done | bytes 442400 | tf_op jit(solution)/shard_map/ppermute | solution.py:1056
  81.5 20.8 %collective-permute-done.15.refs_4_ = bf16[288,384]{1,0:T(8,128)(2,1)S(1)} collective-permute-done((bf16[288,384]{1,0:T(8,128)(2,1)S(1)}, bf16[288,384]{1,0:T(8,128)(2,1)S(1)}, u32[]{:S(2)}, u32[]{:S(2)}) %collective-permute-start.15) | collective-permute-done | bytes 221216 | tf_op jit(solution)/shard_map/ppermute | solution.py:1063
  110.2 8.6 %all-gather.6.cloned.1.call-done = bf16[3584,768]{1,0:T(8,128)(2,1)} async-done(((bf16[112,768]{1,0:T(8,128)(2,1)}), bf16[3584,768]{1,0:T(8,128)(2,1)}) %all-gather.6.cloned.1.call-update) | async-done | bytes 5505040 | tf_op jit(solution)/shard_map/all_gather | solution.py:1052
  120.7 7.2 %project.2 = (bf16[640,768]{1,0:T(8,128)(2,1)}, bf16[3,640,768]{2,1,0:T(8,128)(2,1)}) custom-call(s32[3]{0:T(128)} %pad_add_fusion.at_ref, f32[640,768]{1,0:T(8,128)} %convert_add_fusion.hidden_ref, f32[12,768]{1,0:T(8,128)} %squeeze.60.vec_ref, bf16[4,8,112,768]{3,2,1,0:T(8,128)(2,1)} %bitcast.118), custom_call_target="tpu_custom_call" | custom-call | flops 7699999744 | bytes 1048576 | tf_op jit(solution)/shard_map/project/pallas_call | solution.py:202
  127.8 12.5 %attention.2 = (bf16[640,768]{1,0:T(8,128)(2,1)}, f32[6,640,2]{2,1,0:T(8,128)}) custom-call(bf16[3,640,768]{2,1,0:T(8,128)(2,1)} %get-tuple-element.161.q_ref.k_ref.v_ref, bf16[3,640,768]{2,1,0:T(8,128)(2,1)} %get-tuple-element.161.q_ref.k_ref.v_ref, bf16[3,640,768]{2,1,0:T(8,128)(2,1)} %get-tuple-element.161.q_ref.k_ref.v_ref, ...), custom_call_target="tpu_custom_call" | custom-call | flops 16499999744 | bytes 1048576 | tf_op jit(solution)/shard_map/attention/pallas_call | solution.py:406
  140.4 8.5 %assemble.3.refs_1_.refs_3_ = bf16[2,4,4,96,768]{4,3,2,1,0:T(8,128)(2,1)} custom-call(s32[3]{0:T(128)} %pad_add_fusion.at_ref, bf16[2,4,96,768]{3,2,1,0:T(8,128)(2,1)} %cast.3.own, bf16[288,768]{1,0:T(8,128)(2,1)} %collective-permute-done.refs_0_, bf16[288,768]{1,0:T(8,128)(2,1)} %collective-permute-done.2.refs_1_, ...), custom_call_target="tpu_custom_call" | custom-call | flops 6600000000 | bytes 1048576 | tf_op jit(solution)/shard_map/assemble/pallas_call | solution.py:932
  161.0 17.4 %feed.1 = (bf16[640,768]{1,0:T(8,128)(2,1)}, bf16[640,768]{1,0:T(8,128)(2,1)}, bf16[4,640,768]{2,1,0:T(8,128)(2,1)}, f32[4,640,768]{2,1,0:T(8,128)}, bf16[640,768]{1,0:T(8,128)(2,1)}) custom-call(s32[3]{0:T(128)} %pad_add_fusion.at_ref, f32[640,768]{1,0:T(8,128)} %convert_add_fusion.hidden_ref, bf16[640,768]{1,0:T(8,128)(2,1)} %get-tuple-element.191.o_ref, ...), custom_call_target="tpu_custom_call" | custom-call | flops 18699999232 | bytes 1048576 | tf_op jit(solution)/shard_map/feed/pallas_call | solution.py:253
  183.7 6.9 %project.3 = (bf16[640,768]{1,0:T(8,128)(2,1)}, bf16[3,640,768]{2,1,0:T(8,128)(2,1)}) custom-call(s32[3]{0:T(128)} %pad_add_fusion.at_ref, bf16[640,768]{1,0:T(8,128)(2,1)} %get-tuple-element.193.hidden_ref, f32[12,768]{1,0:T(8,128)} %squeeze.61.vec_ref, bf16[1,4,4,96,768]{4,3,2,1,0:T(8,128)(2,1)} %assemble.4.refs_0_, ...), custom_call_target="tpu_custom_call" | custom-call | flops 7699999744 | bytes 1048576 | tf_op jit(solution)/shard_map/project/pallas_call | solution.py:202
  195.3 8.3 %assemble.5.refs_2_.refs_4_ = bf16[2,4,4,96,768]{4,3,2,1,0:T(8,128)(2,1)} custom-call(s32[3]{0:T(128)} %pad_add_fusion.at_ref, bf16[2,4,96,768]{3,2,1,0:T(8,128)(2,1)} %cast.5.own, bf16[192,768]{1,0:T(8,128)(2,1)} %copy-done.7, bf16[192,768]{1,0:T(8,128)(2,1)} %get-tuple-element.415.refs_1_, bf16[192,768]{1,0:T(8,128)(2,1)} %get-tuple-element.396.refs_2_, ...), custom_call_target="tpu_custom_call" | custom-call | flops 6600000000 | bytes 1048576 | tf_op jit(solution)/shard_map/assemble/pallas_call | solution.py:932
  204.8 12.7 %attention.3 = (bf16[640,768]{1,0:T(8,128)(2,1)}, f32[6,640,2]{2,1,0:T(8,128)}) custom-call(bf16[3,640,768]{2,1,0:T(8,128)(2,1)} %get-tuple-element.201.q_ref.k_ref.v_ref, bf16[3,640,768]{2,1,0:T(8,128)(2,1)} %get-tuple-element.201.q_ref.k_ref.v_ref, bf16[3,640,768]{2,1,0:T(8,128)(2,1)} %get-tuple-element.201.q_ref.k_ref.v_ref, ...), custom_call_target="tpu_custom_call" | custom-call | flops 16499999744 | bytes 1048576 | tf_op jit(solution)/shard_map/attention/pallas_call | solution.py:406
  217.5 34.7 %feed_both.1 = (bf16[640,768]{1,0:T(8,128)(2,1)}, bf16[640,768]{1,0:T(8,128)(2,1)}, bf16[640,768]{1,0:T(8,128)(2,1)}, bf16[640,768]{1,0:T(8,128)(2,1)}, f32[8,76...) custom-call(s32[3]{0:T(128)} %pad_add_fusion.at_ref, ...), custom_call_target="tpu_custom_call" | custom-call | flops 37399998464 | bytes 1048576 | tf_op jit(solution)/shard_map/feed_both/pallas_call | solution.py:607
  254.3 19.3 %attention_back.2.joined_ref = bf16[3,640,768]{2,1,0:T(8,128)(2,1)} custom-call(bf16[3,640,768]{2,1,0:T(8,128)(2,1)} %get-tuple-element.201.q_ref.k_ref.v_ref, bf16[3,640,768]{2,1,0:T(8,128)(2,1)} %get-tuple-element.201.q_ref.k_ref.v_ref, bf16[3,640,768]{2,1,0:T(8,128)(2,1)} %get-tuple-element.201.q_ref.k_ref.v_ref, ...), custom_call_target="tpu_custom_call" | custom-call | flops 20899999744 | bytes 1048576 | tf_op jit(solution)/shard_map/attention_back/pallas_call | solution.py:426
  273.5 8.0 %attention_weights.2 = (bf16[8,2,1,96,384]{4,3,2,1,0:T(8,128)(2,1)}, bf16[8,1,96,384]{3,2,1,0:T(8,128)(2,1)}, bf16[8,1,96,384]{3,2,1,0:T(8,128)(2,1)}) custom-call(s32[3]{0:T(128)} %pad_add_fusion.at_ref, bf16[640,768]{1,0:T(8,128)(2,1)} %get-tuple-element.209.a_ref, bf16[640,768]{1,0:T(8,128)(2,1)} %get-tuple-element.202.o_ref, ...), custom_call_target="tpu_custom_call" | custom-call | flops 8800000000 | bytes 1048576 | tf_op jit(solution)/shard_map/attention_weights/pallas_call | solution.py:798
  283.7 8.8 %project_back.2 = (bf16[640,768]{1,0:T(8,128)(2,1)}, f32[8,768]{1,0:T(8,128)}) custom-call(s32[3]{0:T(128)} %pad_add_fusion.at_ref, bf16[640,768]{1,0:T(8,128)(2,1)} %get-tuple-element.220.up_ref, bf16[640,768]{1,0:T(8,128)(2,1)} %get-tuple-element.193.hidden_ref, f32[12,768]{1,0:T(8,128)} %squeeze.61.vec_ref, ...), custom_call_target="tpu_custom_call" | custom-call | flops 8800000000 | bytes 1048576 | tf_op jit(solution)/shard_map/project_back/pallas_call | solution.py:378
  298.1 7.2 %units_sum.1 = bf16[8,2,3,96,384]{4,3,2,1,0:T(8,128)(2,1)} custom-call(bf16[8,2,1,96,384]{4,3,2,1,0:T(8,128)(2,1)} %get-tuple-element.219.refs_0_, bf16[8,1,96,384]{3,2,1,0:T(8,128)(2,1)} %copy-done.29, bf16[8,1,96,384]{3,2,1,0:T(8,128)(2,1)} %copy-done.30, bf16[8,2,2,96,384]{4,3,2,1,0:T(8,128)(2,1)} %get-tuple-element.225.refs_3_, ...), custom_call_target="tpu_custom_call" | custom-call | flops 6600000000 | bytes 1048576 | tf_op jit(solution)/shard_map/units_sum/pallas_call | solution.py:837
  308.3 24.5 %feed_back_whole.1 = (bf16[640,768]{1,0:T(8,128)(2,1)}, bf16[640,768]{1,0:T(8,128)(2,1)}, bf16[640,768]{1,0:T(8,128)(2,1)}, f32[8,768]{1,0:T(8,128)}, bf16[2,2,4...) custom-call(s32[3]{0:T(128)} %pad_add_fusion.at_ref, bf16[640,768]{1,0:T(8,128)(2,1)} %get-tuple-element.230.up_ref, ...), custom_call_target="tpu_custom_call" | custom-call | flops 24199999488 | bytes 1048576 | tf_op jit(solution)/shard_map/feed_back_whole/pallas_call | solution.py:729
  342.6 18.9 %attention_back.3.joined_ref = bf16[3,640,768]{2,1,0:T(8,128)(2,1)} custom-call(bf16[3,640,768]{2,1,0:T(8,128)(2,1)} %get-tuple-element.161.q_ref.k_ref.v_ref, bf16[3,640,768]{2,1,0:T(8,128)(2,1)} %get-tuple-element.161.q_ref.k_ref.v_ref, bf16[3,640,768]{2,1,0:T(8,128)(2,1)} %get-tuple-element.161.q_ref.k_ref.v_ref, ...), custom_call_target="tpu_custom_call" | custom-call | flops 20899999744 | bytes 1048576 | tf_op jit(solution)/shard_map/attention_back/pallas_call | solution.py:426
  369.3 8.8 %project_back.3 = (bf16[640,768]{1,0:T(8,128)(2,1)}, f32[8,768]{1,0:T(8,128)}) custom-call(s32[3]{0:T(128)} %pad_add_fusion.at_ref, bf16[640,768]{1,0:T(8,128)(2,1)} %get-tuple-element.248.up_ref, f32[640,768]{1,0:T(8,128)} %convert_add_fusion.hidden_ref, f32[12,768]{1,0:T(8,128)} %squeeze.60.vec_ref, bf16[3,640,768]{2,1,0:T(8,128)(2,1)} %attention_back.3.joined_ref, ...), custom_call_target="tpu_custom_call" | custom-call | flops 8800000000 | bytes 1048576 | tf_op jit(solution)/shard_map/project_back/pallas_call | solution.py:378
  380.1 8.6 %collective-permute-done.34 = bf16[2,2,96,384]{3,2,1,0:T(8,128)(2,1)S(1)} collective-permute-done((bf16[2,2,96,384]{3,2,1,0:T(8,128)(2,1)S(1)}, bf16[2,2,96,384]{3,2,1,0:T(8,128)(2,1)S(1)}, u32[]{:S(2)}, u32[]{:S(2)}) %collective-permute-start.34) | collective-permute-done | bytes 294944 | tf_op jit(solution)/shard_map/ppermute | solution.py:1191
  394.4 7.8 %attention_weights.3 = (bf16[2,2,4,1,112,384]{5,4,3,2,1,0:T(8,128)(2,1)}, bf16[2,2,4,1,112,384]{5,4,3,2,1,0:T(8,128)(2,1)}) custom-call(s32[3]{0:T(128)} %pad_add_fusion.at_ref, bf16[640,768]{1,0:T(8,128)(2,1)} %get-tuple-element.252.a_ref, bf16[640,768]{1,0:T(8,128)(2,1)} %get-tuple-element.191.o_ref, bf16[3,640,768]{2,1,0:T(8,128)(2,1)} %attention_back.3.joined_ref, ...), custom_call_target="tpu_custom_call" | custom-call | flops 8800000000 | bytes 1048576 | tf_op jit(solution)/shard_map/attention_weights/pallas_call | solution.py:798
  435.1 7.5 %adam.5 = (f32[2,2,96,3072]{3,2,1,0:T(8,128)}, f32[2,2,96,3072]{3,2,1,0:T(8,128)}, f32[2,2,96,3072]{3,2,1,0:T(8,128)}, f32[2,2,96,3072]{3,2,1,0:T(8,128)}) custom-call(s32[3]{0:T(128)} %pad_add_fusion.at_ref, f32[2]{0:T(128)} %rate_ref.7, bf16[4,2,3,96,384]{4,3,2,1,0:T(8,128)(2,1)} %all-gather.4.cloned.1.call-done.grad_ref, f32[2,2,96,3072]{3,2,1,0:T(8,128)} %weight_ref.12, ...), custom_call_target="tpu_custom_call" | custom-call | flops 6600000000 | bytes 1048576 | tf_op jit(solution)/shard_map/adam/pallas_call | solution.py:886
  453.3 7.2 %adam.6 = (f32[2,2,96,3072]{3,2,1,0:T(8,128)}, f32[2,2,96,3072]{3,2,1,0:T(8,128)}, f32[2,2,96,3072]{3,2,1,0:T(8,128)}, f32[2,2,96,3072]{3,2,1,0:T(8,128)}) custom-call(s32[3]{0:T(128)} %pad_add_fusion.at_ref, f32[2]{0:T(128)} %rate_ref.7, ...), custom_call_target="tpu_custom_call", output_to_operand_aliasing={{0}: (6, {}), {1}: (7, {}), {2}: (8, {}), {3}: (9, {})} | custom-call | flops 6600000000 | bytes 1048576 | tf_op jit(solution)/shard_map/adam/pallas_call | solution.py:886
  (273 shorter events, 162.5 us)
Async XLA Ops:
  7.2 111.6 %all-gather.6.cloned.1.call-start = ((), (), s32[]{:S(2)}) async-start(), calls=%async_computation.3 | async-start | bytes 5677056 | tf_op jit(solution)/shard_map/all_gather | solution.py:1052
  12.6 348.9 %reduce-scatter.2.cloned.1.call-start = ((), (), s32[]{:S(2)}) async-start(), calls=%async_computation.1 | async-start | bytes 3981312 | tf_op jit(solution)/shard_map/reduce_scatter | solution.py:1258
  43.4 30.4 %collective-permute-start.5 = (bf16[288,768]{1,0:T(8,128)(2,1)}, bf16[288,768]{1,0:T(8,128)(2,1)S(1)}, u32[]{:S(2)}, u32[]{:S(2)}) collective-permute-start(bf16[288,768]{1,0:T(8,128)(2,1)} %collective-permute-done.1.refs_5_), channel_id=1, source_target_pairs={{0,8},{8,0},{16,24},{24,16},{1,9},{9,1},{17,25},{25,17},{2,10},{10... | collective-permute-start | bytes 1327112 | tf_op jit(solution)/shard_map/ppermute | solution.py:1059
  44.6 29.2 %collective-permute-start.6 = (bf16[288,768]{1,0:T(8,128)(2,1)}, bf16[288,768]{1,0:T(8,128)(2,1)S(1)}, u32[]{:S(2)}, u32[]{:S(2)}) collective-permute-start(bf16[288,768]{1,0:T(8,128)(2,1)} %collective-permute-done.1.refs_5_), channel_id=1, source_target_pairs={{0,16},{8,24},{16,0},{24,8},{1,17},{9,25},{17,1},{25,9},{2,18},{10... | collective-permute-start | bytes 1327112 | tf_op jit(solution)/shard_map/ppermute | solution.py:1059
  45.7 28.1 %collective-permute-start.4 = (bf16[288,768]{1,0:T(8,128)(2,1)S(1)}, bf16[288,768]{1,0:T(8,128)(2,1)}, u32[]{:S(2)}, u32[]{:S(2)}) collective-permute-start(bf16[288,768]{1,0:T(8,128)(2,1)S(1)} %copy-done.31), channel_id=1, source_target_pairs={{0,4},{1,5},{2,6},{3,7},{4,0},{5,1},{6,2},{7,3},{8,12},{9,13},{10,... | collective-permute-start | bytes 1327112 | tf_op jit(solution)/shard_map/ppermute | solution.py:1056
  51.2 28.7 %collective-permute-start.14 = (bf16[288,384]{1,0:T(8,128)(2,1)S(1)}, bf16[288,384]{1,0:T(8,128)(2,1)S(1)}, u32[]{:S(2)}, u32[]{:S(2)}) collective-permute-start(bf16[288,384]{1,0:T(8,128)(2,1)S(1)} %slice.168), channel_id=1, source_target_pairs={{0,8},{8,0},{16,24},{24,16},{1,9},{9,1},{17,25},{25,17},{2,10},{10... | collective-permute-start | bytes 663560 | tf_op jit(solution)/shard_map/ppermute | solution.py:1062
  73.8 32.6 %collective-permute-start.12 = (bf16[288,768]{1,0:T(8,128)(2,1)}, bf16[288,768]{1,0:T(8,128)(2,1)S(1)}, u32[]{:S(2)}, u32[]{:S(2)}) collective-permute-start(bf16[288,768]{1,0:T(8,128)(2,1)} %collective-permute-done.4.refs_10_), channel_id=1, source_target_pairs={{0,8},{8,0},{16,24},{24,16},{1,9},{9,1},{17,25},{25,17},{2,10},{10... | collective-permute-start | bytes 1327112 | tf_op jit(solution)/shard_map/ppermute | solution.py:1059
  74.4 32.0 %collective-permute-start.13 = (bf16[288,768]{1,0:T(8,128)(2,1)}, bf16[288,768]{1,0:T(8,128)(2,1)S(1)}, u32[]{:S(2)}, u32[]{:S(2)}) collective-permute-start(bf16[288,768]{1,0:T(8,128)(2,1)} %collective-permute-done.4.refs_10_), channel_id=1, source_target_pairs={{0,16},{8,24},{16,0},{24,8},{1,17},{9,25},{17,1},{25,9},{2,18},{10... | collective-permute-start | bytes 1327112 | tf_op jit(solution)/shard_map/ppermute | solution.py:1059
  76.8 25.5 %collective-permute-start.15 = (bf16[288,384]{1,0:T(8,128)(2,1)S(1)}, bf16[288,384]{1,0:T(8,128)(2,1)S(1)}, u32[]{:S(2)}, u32[]{:S(2)}) collective-permute-start(bf16[288,384]{1,0:T(8,128)(2,1)S(1)} %slice.169), channel_id=1, source_target_pairs={{0,16},{8,24},{16,0},{24,8},{1,17},{9,25},{17,1},{25,9},{2,18},{10... | collective-permute-start | bytes 663560 | tf_op jit(solution)/shard_map/ppermute | solution.py:1063
  78.3 24.0 %collective-permute-start.16 = (bf16[288,384]{1,0:T(8,128)(2,1)S(1)}, bf16[288,384]{1,0:T(8,128)(2,1)S(1)}, u32[]{:S(2)}, u32[]{:S(2)}) collective-permute-start(bf16[288,384]{1,0:T(8,128)(2,1)S(1)} %slice.170), channel_id=1, source_target_pairs={{0,8},{8,0},{16,24},{24,16},{1,9},{9,1},{17,25},{25,17},{2,10},{10... | collective-permute-start | bytes 663560 | tf_op jit(solution)/shard_map/ppermute | solution.py:1062
  79.9 26.4 %collective-permute-start.17 = (bf16[288,384]{1,0:T(8,128)(2,1)S(1)}, bf16[288,384]{1,0:T(8,128)(2,1)S(1)}, u32[]{:S(2)}, u32[]{:S(2)}) collective-permute-start(bf16[288,384]{1,0:T(8,128)(2,1)S(1)} %slice.171), channel_id=1, source_target_pairs={{0,16},{8,24},{16,0},{24,8},{1,17},{9,25},{17,1},{25,9},{2,18},{10... | collective-permute-start | bytes 663560 | tf_op jit(solution)/shard_map/ppermute | solution.py:1063
  102.3 38.0 %collective-permute-start.7 = (bf16[192,768]{1,0:T(8,128)(2,1)}, bf16[192,768]{1,0:T(8,128)(2,1)S(1)}, u32[]{:S(2)}, u32[]{:S(2)}) collective-permute-start(bf16[192,768]{1,0:T(8,128)(2,1)} %get-tuple-element.172), channel_id=1, source_target_pairs={{0,2},{1,3},{2,4},{3,5},{4,6},{5,7},{6,0},{7,1},{8,10},{9,11},{10,... | collective-permute-start | bytes 884744 | tf_op jit(solution)/shard_map/ppermute | solution.py:1056
  102.3 38.0 %collective-permute-start.8 = (bf16[192,768]{1,0:T(8,128)(2,1)}, bf16[192,768]{1,0:T(8,128)(2,1)S(1)}, u32[]{:S(2)}, u32[]{:S(2)}) collective-permute-start(bf16[192,768]{1,0:T(8,128)(2,1)} %get-tuple-element.172), channel_id=1, source_target_pairs={{0,6},{1,7},{2,0},{3,1},{4,2},{5,3},{6,4},{7,5},{8,14},{9,15},{10,... | collective-permute-start | bytes 884744 | tf_op jit(solution)/shard_map/ppermute | solution.py:1056
  106.3 34.1 %collective-permute-start.9 = (bf16[192,768]{1,0:T(8,128)(2,1)}, bf16[192,768]{1,0:T(8,128)(2,1)S(1)}, u32[]{:S(2)}, u32[]{:S(2)}) collective-permute-start(bf16[192,768]{1,0:T(8,128)(2,1)} %get-tuple-element.172), channel_id=1, source_target_pairs={{0,4},{1,5},{2,6},{3,7},{4,0},{5,1},{6,2},{7,3},{8,12},{9,13},{10,... | collective-permute-start | bytes 884744 | tf_op jit(solution)/shard_map/ppermute | solution.py:1056
  107.2 33.1 %collective-permute-start.18 = (bf16[288,384]{1,0:T(8,128)(2,1)}, bf16[288,384]{1,0:T(8,128)(2,1)}, u32[]{:S(2)}, u32[]{:S(2)}) collective-permute-start(bf16[288,384]{1,0:T(8,128)(2,1)} %slice.172), channel_id=1, source_target_pairs={{0,8},{8,0},{16,24},{24,16},{1,9},{9,1},{17,25},{25,17},{2,10},{10... | collective-permute-start | bytes 663560 | tf_op jit(solution)/shard_map/ppermute | solution.py:1062
  109.5 31.0 %collective-permute-start.19 = (bf16[288,384]{1,0:T(8,128)(2,1)}, bf16[288,384]{1,0:T(8,128)(2,1)}, u32[]{:S(2)}, u32[]{:S(2)}) collective-permute-start(bf16[288,384]{1,0:T(8,128)(2,1)} %slice.173), channel_id=1, source_target_pairs={{0,16},{8,24},{16,0},{24,8},{1,17},{9,25},{17,1},{25,9},{2,18},{10... | collective-permute-start | bytes 663560 | tf_op jit(solution)/shard_map/ppermute | solution.py:1063
  154.9 28.8 %collective-permute-start.23 = (bf16[1,4,4,96,768]{4,3,2,1,0:T(8,128)(2,1)}, bf16[1,4,4,96,768]{4,3,2,1,0:T(8,128)(2,1)}, u32[]{:S(2)}, u32[]{:S(2)}) collective-permute-start(bf16[1,4,4,96,768]{4,3,2,1,0:T(8,128)(2,1)} %assemble.4.refs_0_), channel_id=1, source_target_pairs={{0,1},{1,0},{2,3},{3,2},{4,5},{5,4},{6,7},{7,6},{8,9},{9,8},{10,11... | collective-permute-start | bytes 7077896 | tf_op jit(solution)/shard_map/ppermute | solution.py:1067
  252.2 29.3 %collective-permute-start.25 = (bf16[8,2,96,384]{3,2,1,0:T(8,128)(2,1)}, bf16[8,2,96,384]{3,2,1,0:T(8,128)(2,1)S(1)}, u32[]{:S(2)}, u32[]{:S(2)}) collective-permute-start(bf16[8,2,96,384]{3,2,1,0:T(8,128)(2,1)} %get-tuple-element.207), channel_id=1, source_target_pairs={{0,8},{8,0},{16,24},{24,16},{1,9},{9,1},{17,25},{25,17},{2,10},{10... | collective-permute-start | bytes 3538952 | tf_op jit(solution)/shard_map/ppermute | solution.py:1246
  252.9 28.6 %collective-permute-start.26 = (bf16[8,2,96,384]{3,2,1,0:T(8,128)(2,1)}, bf16[8,2,96,384]{3,2,1,0:T(8,128)(2,1)S(1)}, u32[]{:S(2)}, u32[]{:S(2)}) collective-permute-start(bf16[8,2,96,384]{3,2,1,0:T(8,128)(2,1)} %get-tuple-element.208), channel_id=1, source_target_pairs={{0,16},{8,24},{16,0},{24,8},{1,17},{9,25},{17,1},{25,9},{2,18},{10... | collective-permute-start | bytes 3538952 | tf_op jit(solution)/shard_map/ppermute | solution.py:1247
  305.3 86.0 %all-gather.4.cloned.1.call-start = ((), (), s32[]{:S(2)}) async-start(), calls=%async_computation.2 | async-start | bytes 2211840 | tf_op jit(solution)/shard_map/all_gather | solution.py:1273
  306.8 26.1 %collective-permute-start.29 = (bf16[640,192]{1,0:T(8,128)(2,1)S(1)}, bf16[640,192]{1,0:T(8,128)(2,1)S(1)}, u32[]{:S(2)}, u32[]{:S(2)}) collective-permute-start(bf16[640,192]{1,0:T(8,128)(2,1)S(1)} %get-tuple-element.393), channel_id=1, source_target_pairs={{0,8},{8,0},{16,24},{24,16},{1,9},{9,1},{17,25},{25,17},{2,10},{10... | collective-permute-start | bytes 737288 | tf_op jit(solution)/shard_map/ppermute | solution.py:1172
  365.5 23.1 %collective-permute-start.34 = (bf16[2,2,96,384]{3,2,1,0:T(8,128)(2,1)S(1)}, bf16[2,2,96,384]{3,2,1,0:T(8,128)(2,1)S(1)}, u32[]{:S(2)}, u32[]{:S(2)}) collective-permute-start(bf16[2,2,96,384]{3,2,1,0:T(8,128)(2,1)S(1)} %get-tuple-element.388), channel_id=1, source_target_pairs={{0,4},{1,5},{2,6},{3,7},{4,0},{5,1},{6,2},{7,3},{8,12},{9,13},{10,... | collective-permute-start | bytes 884744 | tf_op jit(solution)/shard_map/ppermute | solution.py:1191
  365.6 23.0 %collective-permute-start.35 = (bf16[2,2,96,384]{3,2,1,0:T(8,128)(2,1)S(1)}, bf16[2,2,96,384]{3,2,1,0:T(8,128)(2,1)S(1)}, u32[]{:S(2)}, u32[]{:S(2)}) collective-permute-start(bf16[2,2,96,384]{3,2,1,0:T(8,128)(2,1)S(1)} %get-tuple-element.387), channel_id=1, source_target_pairs={{0,6},{1,7},{2,0},{3,1},{4,2},{5,3},{6,4},{7,5},{8,14},{9,15},{10,... | collective-permute-start | bytes 884744 | tf_op jit(solution)/shard_map/ppermute | solution.py:1191
  428.2 22.3 %collective-permute-start.47 = (bf16[2,2,96,384]{3,2,1,0:T(8,128)(2,1)S(1)}, bf16[2,2,96,384]{3,2,1,0:T(8,128)(2,1)S(1)}, u32[]{:S(2)}, u32[]{:S(2)}) collective-permute-start(bf16[2,2,96,384]{3,2,1,0:T(8,128)(2,1)S(1)} %fusion.7), channel_id=1, source_target_pairs={{0,16},{8,24},{16,0},{24,8},{1,17},{9,25},{17,1},{25,9},{2,18},{10... | collective-permute-start | bytes 884744 | tf_op jit(solution)/shard_map/ppermute | solution.py:1204
  (64 other events, 977.2 us)
Sparse Core Ops, SparseCore 0:
  12.8 105.9 all-gather.5
  305.5 41.0 reduce-scatter.1
  361.7 29.5 all-gather.3
